TPU v7x, 256 devices: a whole 4x4x8 slice. The times are simulated.
256 devices in a mesh: pipe: 8 (over y, x_lo), expert: 32 (over z, x_hi, core).
Axes of the slice: x: 4 (x_hi: 2, x_lo: 2; x = x_hi * 2 + x_lo), y: 4, z: 8, core: 2. Of those that a mesh axis runs over, the one named last changes fastest.
Arguments:
- fwd_tokens: bfloat16 [8, 2048, 3584], P('pipe', 'expert'), may hold values from -6 to 6
- bwd_tokens: bfloat16 [8, 2048, 3584], P('pipe', 'expert'), may hold values from -6 to 6
- routes: int32 [8, 32, 128, 2], P('pipe', 'expert'), may hold values from 0 to 15, all different within a row; in each aligned block of 128 rows (0 to 127, 128 to 255, ..., all dimensions but the last counted through in order) at most 20 rows name the same one
- route_weights: float32 [8, 32, 128, 2], P('pipe', 'expert'), may hold values from 0.2 to 1
- norm_gain: float32 [8, 3584], P('pipe'), may hold values from 0.5 to 1.5
- gate_up: bfloat16 [8, 32, 3584, 1024], P('pipe', 'expert'), may hold values from -0.09375 to 0.09375
- down: bfloat16 [8, 32, 512, 3584], P('pipe', 'expert'), may hold values from -0.1875 to 0.1875
Outputs:
- fwd_next: bfloat16 [8, 2048, 3584], P('pipe', 'expert')
- bwd_next: bfloat16 [8, 2048, 3584], P('pipe', 'expert')
Inputs may be any that keep to these rules, and one draw needn't show every extreme that they name: In each block [s, e] of 128 rows at most 20 routes name one expert, and some block reaches 20; a token's 2 routes name different experts.
All inputs are finite; a program needn't handle non-finite values.
Results may differ from a plain program's by a relative error of at most 0.0049.
Values may be sent and summed in bfloat16 or wider, within the bound.
No kernel may reach another device: no remote copies, remote signals or barrier semaphores. Data moves between devices by JAX's collectives and lax.ppermute only.
A program may use at most 64 MiB of HBM per device.

v0:
```python
import jax
import jax.numpy as jnp
from jax import lax
from jax.sharding import PartitionSpec as P


def shifted(block, axis, distance):
    devices = range(lax.axis_size(axis))
    route = [((i - distance) % len(devices), i) for i in devices]
    return lax.ppermute(block, axis, route)


def rms_rows(rows, gain):
    values = rows.astype(jnp.float32)
    scale = lax.rsqrt(jnp.mean(values * values, axis=-1, keepdims=True) + 1e-06)
    return (values * scale * gain).astype(jnp.bfloat16)


def slot_ranks(route_ids, experts):
    flat_ids = route_ids.reshape(-1)
    onehot = (flat_ids[:, None] == jnp.arange(experts, dtype=jnp.int32)[None, :]).astype(jnp.int32)
    earlier = jnp.cumsum(onehot, axis=0) - onehot
    return jnp.sum(earlier * onehot, axis=1)


def expert_rows(received, weights_up, weights_down):
    groups, slots, width = received.shape
    hidden_half = weights_down.shape[0]
    flat_rows = received.reshape(groups * slots, width)
    pre = jnp.dot(flat_rows, weights_up, preferred_element_type=jnp.float32)
    hidden = (jax.nn.silu(pre[:, :hidden_half]) * pre[:, hidden_half:]).astype(jnp.bfloat16)
    result = jnp.dot(hidden, weights_down, preferred_element_type=jnp.float32).astype(jnp.bfloat16)
    return result.reshape(groups, slots, width)


def on_device(fwd_tokens, bwd_tokens, routes, route_weights, norm_gain, gate_up, down):
    width = fwd_tokens.shape[2]
    half_rows = fwd_tokens.shape[1]
    rows = jnp.concatenate([fwd_tokens[0], bwd_tokens[0]], axis=0)
    tok_rows = rows.shape[0]
    normed = rms_rows(rows, norm_gain[0])
    route_ids = routes[0, 0]
    top = route_ids.shape[1]
    devices = lax.axis_size("expert")
    experts = devices // 2
    capacity = min(tok_rows, 5 * tok_rows * top // (2 * devices))
    flat_ids = route_ids.reshape(-1)
    ranks = slot_ranks(route_ids, experts)
    owners = jnp.arange(flat_ids.shape[0], dtype=jnp.int32) // top + 1
    match = (flat_ids[:, None, None] == jnp.arange(experts, dtype=jnp.int32)[None, :, None]) & (
        ranks[:, None, None] == jnp.arange(capacity, dtype=jnp.int32)[None, None, :]
    )
    slot_owner = jnp.sum(match.astype(jnp.int32) * owners[:, None, None], axis=0) - 1
    valid = slot_owner >= 0
    picked = normed[jnp.maximum(slot_owner, 0)]
    picked = jnp.where(valid[:, :, None], picked, jnp.zeros_like(picked))
    outgoing = jnp.repeat(picked, 2, axis=0)
    weights_up = gate_up[0, 0]
    weights_down = down[0, 0]
    received = lax.all_to_all(outgoing, "expert", split_axis=0, concat_axis=0, tiled=True)
    results = expert_rows(received, weights_up, weights_down)
    returned = lax.all_to_all(results, "expert", split_axis=0, concat_axis=0, tiled=True)
    by_expert = returned.reshape(experts, 2, capacity, width)
    combined = by_expert[:, 0].astype(jnp.float32) + by_expert[:, 1].astype(jnp.float32)
    chosen = combined[flat_ids, ranks].reshape(tok_rows, top, width)
    mixed = jnp.sum(route_weights[0, 0][..., None] * chosen, axis=1)
    updated = (rows.astype(jnp.float32) + mixed).astype(jnp.bfloat16)
    fwd_next = shifted(updated[None, :half_rows], "pipe", 1)
    bwd_next = shifted(updated[None, half_rows:], "pipe", -1)
    return (fwd_next, bwd_next)


def solution(mesh):
    in_specs = (
        P("pipe", "expert", None),
        P("pipe", "expert", None),
        P("pipe", "expert", None, None),
        P("pipe", "expert", None, None),
        P("pipe", None),
        P("pipe", "expert", None, None),
        P("pipe", "expert", None, None),
    )
    out_specs = (P("pipe", "expert", None), P("pipe", "expert", None))
    return jax.shard_map(
        on_device, mesh=mesh, in_specs=in_specs, out_specs=out_specs, check_vma=False
    )
```

profile of v0, /device:TPU:1, one launch (start us, length us, event | category | flops | bytes accessed | tf_op | source)
XLA Modules:
  0.0 362.7 jit_solution(7622616457104035455)
XLA Ops:
  0.6 0.8 copy.39
  1.4 0.1 eq.55
  1.6 0.1 eq.59
  1.7 0.6 reduce-window.6
  2.3 0.2 slice_reduce_fusion
  2.6 0.1 fusion.12
  2.7 0.4 select_reduce_fusion
  3.1 0.1 copy.42
  3.2 1.4 fusion.3
  4.6 0.1 reshape.177
  4.7 0.8 reduce.1
  5.5 1.4 fusion.5
  6.9 3.1 gather_fusion
  10.1 2.2 reshape.176
  12.3 2.0 broadcast_select_fusion
  14.3 0.4 broadcast_in_dim.18
  14.8 137.1 %all_to_all.10 = bf16[32,20,3584]{2,1,0:T(8,128)(2,1)} all-to-all(bf16[32,20,3584]{2,1,0:T(8,128)(2,1)S(1)} %bitcast.45), channel_id=1, replica_groups=mesh['pipe'=8,'expert'=32] {'expert'}, dimensions={0} | all-to-all | bytes 9175040 | tf_op jit(solution)/shard_map/all_to_all | solution.py:60
  151.9 7.3 %reshape.171 = bf16[640,3584]{1,0:T(8,128)(2,1)} reshape(bf16[32,20,3584]{2,1,0:T(8,128)(2,1)} %all_to_all.10) | data formatting | bytes 9175040 | tf_op jit(solution)/shard_map/reshape | solution.py:29
  159.1 0.0 copy-start.3
  159.1 8.6 %fusion = f32[640,1024]{1,0:T(8,128)S(1)} fusion(bf16[640,3584]{1,0:T(8,128)(2,1)} %reshape.171, bf16[1,1,3584,1024]{3,2,1,0:T(8,128)(2,1)} %param.12), kind=kOutput, calls=%fused_computation.2 | convolution fusion | flops 4697620480 | bytes 14548992 | tf_op jit(solution)/shard_map/dot_general | solution.py:30
  167.8 0.0 copy-done.3
  167.8 4.8 %convolution_convert_fusion = bf16[640,3584]{1,0:T(8,128)(2,1)} fusion(bf16[1,1,512,3584]{3,2,1,0:T(8,128)(2,1)S(1)} %copy-done.3, f32[640,1024]{1,0:T(8,128)S(1)} %fusion), kind=kOutput, calls=%fused_computation.4 | convolution fusion | flops 2353070080 | bytes 10878976 | tf_op jit(solution)/shard_map/dot_general | solution.py:32
  172.5 7.2 %reshape.172 = bf16[32,20,3584]{2,1,0:T(8,128)(2,1)} reshape(bf16[640,3584]{1,0:T(8,128)(2,1)} %convolution_convert_fusion) | data formatting | bytes 9175040 | tf_op jit(solution)/shard_map/reshape | solution.py:33
  179.8 0.0 copy-start.2
  179.8 6.1 %all-to-all-start.1 = ((bf16[32,20,3584]{2,1,0:T(8,128)(2,1)}), bf16[32,20,3584]{2,1,0:T(8,128)(2,1)}, u32[]{:S(2)}, u32[]{:S(2)}) async-start(bf16[32,20,3584]{2,1,0:T(8,128)(2,1)} %reshape.172), calls=%async_computation.1 | async-start | bytes 11010048 | tf_op jit(solution)/shard_map/all_to_all | solution.py:62
  185.9 0.1 reshape_squeeze.3
  186.0 0.0 copy-done.2
  186.0 0.1 copy.38
  186.2 124.5 %all-to-all-done.1 = bf16[32,20,3584]{2,1,0:T(8,128)(2,1)} async-done(((bf16[32,20,3584]{2,1,0:T(8,128)(2,1)}), bf16[32,20,3584]{2,1,0:T(8,128)(2,1)}, u32[]{:S(2)}, u32[]{:S(2)}) %all-to-all-start.1) | async-done | bytes 4587552 | tf_op jit(solution)/shard_map/all_to_all | solution.py:62
  310.7 3.0 fusion.21
  313.7 3.4 add_bitcast_fusion
  317.0 6.9 %gather_fusion.1 = f32[256,3584]{1,0:T(8,128)} fusion(f32[16,20,3584]{2,0,1:T(8,128)} %add_bitcast_fusion, s32[256]{0:T(256)S(1)} %bitcast.46), kind=kCustom, calls=%fused_computation.1 | custom fusion | bytes 7342080 | tf_op jit(solution)/shard_map/gather | solution.py:65
  324.0 5.5 %reshape.174 = f32[128,2,3584]{2,1,0:T(2,128)} reshape(f32[256,3584]{1,0:T(8,128)} %gather_fusion.1) | data formatting | bytes 7340032 | tf_op jit(solution)/shard_map/reshape | solution.py:65
  329.5 0.0 copy-start
  329.5 0.0 copy-start.1
  329.5 7.4 %multiply_reduce_fusion = f32[128,3584]{1,0:T(8,128)S(1)} fusion(f32[128,2,3584]{2,1,0:T(2,128)} %reshape.174, f32[128,2]{1,0:T(8,128)S(1)} %copy.38), kind=kLoop, calls=%fused_computation.7 | loop fusion | flops 1376256 | bytes 5506048 | tf_op jit(solution)/shard_map/reduce_sum | solution.py:66
  336.9 0.0 copy-done
  336.9 0.0 copy-done.1
  336.9 0.2 fusion.6
  337.1 0.1 slice_bitcast_fusion
  337.1 2.9 collective-permute-start.1
  340.0 0.0 collective-permute-start
  340.0 9.4 %collective-permute-done.1 = bf16[1,64,3584]{2,1,0:T(8,128)(2,1)S(1)} collective-permute-done((bf16[1,64,3584]{2,1,0:T(8,128)(2,1)S(1)}, bf16[1,64,3584]{2,1,0:T(8,128)(2,1)S(1)}, u32[]{:S(2)}, u32[]{:S(2)}) %collective-permute-start.1) | collective-permute-done | bytes 458784 | tf_op jit(solution)/shard_map/ppermute | solution.py:10
  349.4 11.7 %collective-permute-done = bf16[1,64,3584]{2,1,0:T(8,128)(2,1)S(1)} collective-permute-done((bf16[1,64,3584]{2,1,0:T(8,128)(2,1)S(1)}, bf16[1,64,3584]{2,1,0:T(8,128)(2,1)S(1)}, u32[]{:S(2)}, u32[]{:S(2)}) %collective-permute-start) | collective-permute-done | bytes 458784 | tf_op jit(solution)/shard_map/ppermute | solution.py:10
  361.1 0.8 copy.58
  361.9 0.8 copy.59
  (11 shorter events, 0.1 us)
Async XLA Ops:
  159.1 8.6 %copy-start.3 = (bf16[1,1,512,3584]{3,2,1,0:T(8,128)(2,1)S(1)}, bf16[1,1,512,3584]{3,2,1,0:T(8,128)(2,1)}, u32[]{:S(2)}) copy-start(bf16[1,1,512,3584]{3,2,1,0:T(8,128)(2,1)} %param.13) | copy-start | bytes 11010052
  179.8 6.3 %copy-start.2 = (f32[1,1,128,2]{2,3,1,0:T(2,128)S(1)}, f32[1,1,128,2]{2,3,1,0:T(2,128)}, u32[]{:S(2)}) copy-start(f32[1,1,128,2]{2,3,1,0:T(2,128)} %param.10) | copy-start | bytes 3076
  179.8 130.9 %all-to-all-start.1 = ((bf16[32,20,3584]{2,1,0:T(8,128)(2,1)}), bf16[32,20,3584]{2,1,0:T(8,128)(2,1)}, u32[]{:S(2)}, u32[]{:S(2)}) async-start(bf16[32,20,3584]{2,1,0:T(8,128)(2,1)} %reshape.172), calls=%async_computation.1 | async-start | bytes 11010048 | tf_op jit(solution)/shard_map/all_to_all | solution.py:62
  329.5 7.4 %copy-start = (bf16[1,64,3584]{2,1,0:T(8,128)(2,1)S(1)}, bf16[1,64,3584]{2,1,0:T(8,128)(2,1)}, u32[]{:S(2)}) copy-start(bf16[1,64,3584]{2,1,0:T(8,128)(2,1)} %param.8) | copy-start | bytes 1376260
  329.5 7.4 %copy-start.1 = (bf16[1,64,3584]{2,1,0:T(8,128)(2,1)S(1)}, bf16[1,64,3584]{2,1,0:T(8,128)(2,1)}, u32[]{:S(2)}) copy-start(bf16[1,64,3584]{2,1,0:T(8,128)(2,1)} %param.7) | copy-start | bytes 1376260
  337.1 12.3 %collective-permute-start.1 = (bf16[1,64,3584]{2,1,0:T(8,128)(2,1)S(1)}, bf16[1,64,3584]{2,1,0:T(8,128)(2,1)S(1)}, u32[]{:S(2)}, u32[]{:S(2)}) collective-permute-start(bf16[1,64,3584]{2,1,0:T(8,128)(2,1)S(1)} %get-tuple-element.4), channel_id=1, source_target_pairs={{32,0},{64,32},{96,64},{128,96},{160,128},{192,160},{224,192},{0,2... | collective-permute-start | bytes 1376264 | tf_op jit(solution)/shard_map/ppermute | solution.py:10
  340.0 21.1 %collective-permute-start = (bf16[1,64,3584]{2,1,0:T(8,128)(2,1)S(1)}, bf16[1,64,3584]{2,1,0:T(8,128)(2,1)S(1)}, u32[]{:S(2)}, u32[]{:S(2)}) collective-permute-start(bf16[1,64,3584]{2,1,0:T(8,128)(2,1)S(1)} %get-tuple-element.5), channel_id=1, source_target_pairs={{224,0},{0,32},{32,64},{64,96},{96,128},{128,160},{160,192},{192,2... | collective-permute-start | bytes 1376264 | tf_op jit(solution)/shard_map/ppermute | solution.py:10
where the time goes:
time: 363 us
  waiting for transfers between devices  146 us (40%)
  blocking collectives  137 us (38%)
  local copies, waits for them, and re-layouts  39 us (11%)
  other arithmetic  17.8 us (5%)
  matrix products  13.4 us (4%)
  starting transfers between devices  8.98 us (2%)
    all_to_all x1, blocking collectives, on_device(): lax.all_to_all(outgoing, 'expert', split_axis=0, concat_axis=0, tiled=True)  137 us
    all_to_all x1, waiting for transfers between devices, on_device(): lax.all_to_all(results, 'expert', split_axis=0, concat_axis=0, tiled=True)  125 us
    ppermute x2, waiting for transfers between devices, shifted(): return lax.ppermute(block, axis, route)  21.1 us
    dot_general x1, matrix products, expert_rows(): pre = jnp.dot(flat_rows, weights_up, preferred_element_type=jnp.float32)  8.63 us
    reduce_sum x1, other arithmetic, on_device(): mixed = jnp.sum(route_weights[0, 0][..., None] * chosen, axis=1)  7.4 us
    reshape x1, local copies, waits for them, and re-layouts, expert_rows(): flat_rows = received.reshape(groups * slots, width)  7.26 us
  transfers between devices with their start and end apart: 3, of which 3 were waited for; matrix products, arithmetic and copies ran while one was open for 0% of the time, Pallas kernels for 0%

commit v1 on v0

v1 whole, which is shorter than its diff:
```python
import functools
import jax
import jax.numpy as jnp
from jax import lax
from jax.experimental import pallas as pl
from jax.experimental.pallas import tpu as pltpu
from jax.sharding import PartitionSpec as P

D = 3584
H2 = 512
TOK = 128
HALF = 64
CHIPS = 16
MAIN = 16
REST = 4
QUART = D // 4
WIDE = D + QUART
META = 16
PART = H2 // 2
ORDER = ((1, 0), (4, 1), (7, 0), (3, 0), (0, 1), (5, 0), (2, 0), (6, 1), (4, 0), (1, 1), (7, 1), (3, 1), (5, 1), (2, 1), (6, 0), (0, 0))
VMEM = pl.BlockSpec(memory_space=pltpu.VMEM)
HBM = pl.BlockSpec(memory_space=pltpu.HBM)
SMEM = pl.BlockSpec(memory_space=pltpu.SMEM)
F32 = jnp.float32
BF16 = jnp.bfloat16


def iota(shape, axis):
    return lax.broadcasted_iota(jnp.int32, shape, axis)


def call(kernel, out_shape, in_specs, out_specs, scratch=(), limit=24):
    return pl.pallas_call(
        kernel,
        out_shape=out_shape,
        in_specs=in_specs,
        out_specs=out_specs,
        scratch_shapes=scratch,
        compiler_params=pltpu.CompilerParams(vmem_limit_bytes=limit * 2**20),
    )


def build_kernel(place, fwd, bwd, ids_hbm, weights_hbm, gain_hbm, *refs):
    send, carried, ids, weights, gain, packed, sems = refs
    loads = [
        pltpu.make_async_copy(source, target, sems.at[at])
        for at, (source, target) in enumerate(
            ((ids_hbm, ids), (weights_hbm, weights), (gain_hbm, gain), (fwd, carried.at[0:HALF, :]), (bwd, carried.at[HALF:TOK, :]))
        )
    ]
    for load in loads:
        load.start()
    for load in loads[:2]:
        load.wait()
    expert = iota((CHIPS, TOK), 0)
    hits = [expert == ids[k : k + 1, :] for k in range(2)]
    named = jnp.where(hits[0] | hits[1], 1.0, 0.0).astype(BF16)
    before = (iota((TOK, TOK), 0) < iota((TOK, TOK), 1)).astype(BF16)
    counts = jnp.dot(named, before, preferred_element_type=F32)
    ranks = [jnp.sum(jnp.where(hit, counts, 0.0), axis=0, keepdims=True) for hit in hits]
    numbers = []
    for k in range(2):
        dz, dx = ((ids[k : k + 1, :] >> 1) - place[0]) & 7, (ids[k : k + 1, :] & 1) ^ place[1]
        number = jnp.zeros_like(dz)
        for i, (one_z, one_x) in enumerate(ORDER):
            number = jnp.where((dz == one_z) & (dx == one_x), i, number)
        numbers.append(number)
    high = weights[...].astype(BF16).astype(F32)
    low = weights[...] - high
    sub = iota((META, TOK), 0)
    table = jnp.zeros((META, TOK), F32)
    entries = [numbers[0].astype(F32), numbers[1].astype(F32), *ranks, high[0:1], high[1:2], low[0:1], low[1:2]]
    for at, row in enumerate(entries):
        table = jnp.where(sub == at, row, table)
    carried[TOK : TOK + META, :] = jnp.zeros((META, D), BF16)
    carried[TOK : TOK + META, 0:TOK] = table.astype(BF16)
    main, rest = slot_masks([ids[k : k + 1, :] for k in range(2)], [r.astype(jnp.int32) for r in ranks], TOK)
    pick = jnp.where(main[0] | main[1], 1.0, 0.0).astype(BF16)
    picks = [jnp.where(rest[j][0] | rest[j][1], 1.0, 0.0).astype(BF16) for j in range(4)]
    for load in loads[2:]:
        load.wait()
    values = carried[0:TOK, :].astype(F32)
    scale = lax.rsqrt(jnp.mean(values * values, axis=-1, keepdims=True) + 1e-06)
    normed = (values * scale * gain[...]).astype(BF16)
    stores = []
    extra = jnp.zeros((CHIPS * MAIN, QUART), F32)
    for j in range(5):
        cols = slice(j * QUART, (j + 1) * QUART)
        if j < 4:
            packed[:, cols] = jnp.dot(pick, normed[:, cols], preferred_element_type=F32).astype(BF16)
            extra += jnp.dot(picks[j], normed[:, cols], preferred_element_type=F32)
        else:
            packed[:, cols] = extra.astype(BF16)
        stores.append(pltpu.make_async_copy(packed.at[:, cols], send.at[:, cols], sems.at[5 + j]))
        stores[-1].start()
    for store in stores:
        store.wait()


def slot_masks(blocks, ranks, tokens):
    main, rest = [], [[] for _ in range(4)]
    row = iota((CHIPS * MAIN, tokens), 0)
    for block, rank in zip(blocks, ranks):
        main.append(row == jnp.where(rank < MAIN, block * MAIN + rank, -1))
        for j in range(4):
            rest[j].append(row == jnp.where(rank < MAIN, -1, block * MAIN + j * REST + rank - MAIN))
    return main, rest


def build(place, *arrays):
    shape = jax.ShapeDtypeStruct
    return call(
        build_kernel,
        [pltpu.HBM((CHIPS * MAIN, WIDE), BF16), shape((TOK + META, D), BF16)],
        [SMEM] + [HBM] * 5,
        [HBM, VMEM],
        [
            pltpu.VMEM((2, TOK), jnp.int32),
            pltpu.VMEM((2, TOK), F32),
            pltpu.VMEM((1, D), F32),
            pltpu.VMEM((CHIPS * MAIN, WIDE), BF16),
            pltpu.SemaphoreType.DMA((10,)),
        ],
    )(place, *(pltpu.with_memory_space_constraint(a, pltpu.HBM) for a in arrays))


def expert_kernel(place, recv, *refs):
    ups, downs, outs = refs[0:2], refs[2:4], refs[4 : 4 + CHIPS]
    x, tails, total, wide, deep, sems = refs[4 + CHIPS :]
    rows, few = CHIPS * MAIN, CHIPS * REST

    def loads(c):
        w, at, slot = c // 2, (c % 2) * PART, c % 2
        pairs = (
            (ups[w].at[:, at : at + PART], wide.at[slot, :, 0:PART]),
            (ups[w].at[:, H2 + at : H2 + at + PART], wide.at[slot, :, PART : 2 * PART]),
            (downs[w].at[at : at + PART, :], deep.at[slot]),
        )
        return [pltpu.make_async_copy(source, target, sems.at[slot, n]) for n, (source, target) in enumerate(pairs)]

    for c in range(2):
        for load in loads(c):
            load.start()
    for i, (dz, dx) in enumerate(ORDER):
        at = pl.ds(pl.multiple_of((((place[0] - dz) & 7) * 2 + (place[1] ^ dx)) * MAIN, MAIN), MAIN)
        x[i * MAIN : (i + 1) * MAIN, :] = recv[at, 0:D]
        tails[i * MAIN : (i + 1) * MAIN, :] = recv[at, D:WIDE]
    row, col = iota((few, rows), 0), iota((few, rows), 1)
    start = (row // REST) * MAIN + row % REST
    for j in range(4):
        pick = (col == start + j * REST).astype(BF16)
        x[rows:, j * QUART : (j + 1) * QUART] = jnp.dot(pick, tails[...], preferred_element_type=F32).astype(BF16)
    for c in range(4):
        arrived = loads(c)
        arrived[0].wait()
        arrived[1].wait()
        pre = jnp.dot(x[...], wide[c % 2], preferred_element_type=F32)
        gate, value = pre[:, :PART], pre[:, PART:]
        hidden = (gate / (1.0 + jnp.exp(-gate)) * value).astype(BF16)
        arrived[2].wait()
        part = jnp.dot(hidden, deep[c % 2], preferred_element_type=F32)
        if c == 0:
            total[...] = part
        else:
            total[...] += part
        if c < 2:
            for load in loads(c + 2):
                load.start()
    row, col = iota((rows, few), 0), iota((rows, few), 1)
    start = (col // REST) * MAIN + col % REST
    picks = jnp.concatenate([(row == start + j * REST).astype(BF16) for j in range(4)], axis=1)
    rest = jnp.concatenate([total[rows:, j * QUART : (j + 1) * QUART] for j in range(4)], axis=0).astype(BF16)
    extra = jnp.dot(picks, rest, preferred_element_type=F32).astype(BF16)
    for i in range(CHIPS):
        outs[i][:, 0:D] = total[i * MAIN : (i + 1) * MAIN, :].astype(BF16)
        outs[i][:, D:WIDE] = extra[i * MAIN : (i + 1) * MAIN, :]


def expert(place, recv, ups, downs):
    shape = jax.ShapeDtypeStruct
    return call(
        expert_kernel,
        [shape((MAIN, WIDE), BF16)] * CHIPS,
        [SMEM, VMEM] + [HBM] * 4,
        [VMEM] * CHIPS,
        [
            pltpu.VMEM((CHIPS * (MAIN + REST), D), BF16),
            pltpu.VMEM((CHIPS * MAIN, QUART), BF16),
            pltpu.VMEM((CHIPS * (MAIN + REST), D), F32),
            pltpu.VMEM((2, D, 2 * PART), BF16),
            pltpu.VMEM((2, PART, D), BF16),
            pltpu.SemaphoreType.DMA((2, 3)),
        ],
        limit=32,
    )(place, recv, *(pltpu.with_memory_space_constraint(w, pltpu.HBM) for w in (*ups, *downs)))


def combine_kernel(carried, *refs):
    blocks, outs, main_all, rest_all = refs[:CHIPS], refs[CHIPS : CHIPS + 2], refs[CHIPS + 2], refs[CHIPS + 3]
    meta = carried[TOK : TOK + META, 0:TOK].astype(F32)
    numbers = [meta[k : k + 1, :].astype(jnp.int32) for k in range(2)]
    ranks = [meta[2 + k : 3 + k, :].astype(jnp.int32) for k in range(2)]
    main, rest = slot_masks(numbers, ranks, TOK)
    for i in range(CHIPS):
        main_all[i * MAIN : (i + 1) * MAIN, :] = blocks[i][:, 0:D]
        rest_all[i * MAIN : (i + 1) * MAIN, :] = blocks[i][:, D:WIDE]

    def weighed(masks):
        both = []
        for part in range(2):
            w = [meta[4 + 2 * part + k : 5 + 2 * part + k, :] for k in range(2)]
            both.append((jnp.where(masks[0], w[0], 0.0) + jnp.where(masks[1], w[1], 0.0)).astype(BF16))
        return both

    def product(mats, rows):
        dims = (((0,), (0,)), ((), ()))
        return sum(lax.dot_general(m, rows, dims, preferred_element_type=F32) for m in mats)

    main_w = weighed(main)
    for j in range(4):
        cols = slice(j * QUART, (j + 1) * QUART)
        mixed = product(main_w, main_all[:, cols]) + product(weighed(rest[j]), rest_all[...])
        updated = (carried[0:TOK, cols].astype(F32) + mixed).astype(BF16)
        outs[0][:, cols] = updated[0:HALF]
        outs[1][:, cols] = updated[HALF:TOK]


def combine(carried, blocks):
    return call(
        combine_kernel,
        [jax.ShapeDtypeStruct((HALF, D), BF16)] * 2,
        [VMEM] * (CHIPS + 1),
        [VMEM] * 2,
        [pltpu.VMEM((CHIPS * MAIN, D), BF16), pltpu.VMEM((CHIPS * MAIN, QUART), BF16)],
    )(carried, *blocks)


def moved(block, route):
    pairs = []
    for p in range(8):
        for e in range(32):
            q, z, xh, c = route(p, e // 4, (e // 2) % 2, e % 2)
            pairs.append((p * 32 + e, (q % 8) * 32 + (z % 8) * 4 + (xh % 2) * 2 + c))
    return lax.ppermute(block, ("pipe", "expert"), pairs)


def after(block, *ended):
    return lax.optimization_barrier((block, *ended))[0]


def on_device(fwd_tokens, bwd_tokens, routes, route_weights, norm_gain, gate_up, down):
    spot = lax.axis_index("expert")
    place = jnp.stack([spot // 4, (spot // 2) % 2]).astype(jnp.int32)
    send, carried = build(place, fwd_tokens[0], bwd_tokens[0], routes[0, 0].T, route_weights[0, 0].T, norm_gain)
    same_core = [[2 * i + c for i in range(CHIPS)] for c in range(2)]
    recv = lax.all_to_all(send, "expert", split_axis=0, concat_axis=0, tiled=True, axis_index_groups=same_core)
    beside = moved(carried, lambda p, z, xh, c: (p + 1 - 2 * c, z, xh, c))
    ups, downs = ([w, moved(after(w, carried), lambda p, z, xh, c: (p, z, xh, 1 - c))] for w in (gate_up[0, 0], down[0, 0]))
    recv, beside, ups, downs = lax.optimization_barrier((recv, beside, ups, downs))
    back = []
    for (dz, dx), block in zip(ORDER, expert(place, recv, ups, downs)):
        back.append(moved(block, lambda p, z, xh, c, dz=dz, dx=dx: (p + 1 - 2 * c, z - dz, xh + dx, c)))
    fwd, bwd = combine(beside, back)
    fwd_next = moved(fwd, lambda p, z, xh, c: (p + 2 * c, z, xh, c))
    bwd_next = moved(bwd, lambda p, z, xh, c: (p - 2 + 2 * c, z, xh, c))
    return fwd_next[None], bwd_next[None]


def solution(mesh):
    in_specs = (
        P("pipe", "expert", None),
        P("pipe", "expert", None),
        P("pipe", "expert", None, None),
        P("pipe", "expert", None, None),
        P("pipe", None),
        P("pipe", "expert", None, None),
        P("pipe", "expert", None, None),
    )
    out_specs = (P("pipe", "expert", None), P("pipe", "expert", None))
    return jax.shard_map(on_device, mesh=mesh, in_specs=in_specs, out_specs=out_specs, check_vma=False)
```

time: 363 us -> 159 us (0.44)
  blocking collectives: 137 us -> 0 us
  waiting for transfers between devices: 146 us -> 70.5 us
  starting transfers between devices: 8.98 us -> 68 us
  local copies, waits for them, and re-layouts: 39 us -> 2.51 us
  other arithmetic: 17.8 us -> 0.08 us
  Pallas kernels: 0 us -> 17.2 us
  matrix products: 13.4 us -> 0 us
    all_to_all x1 -> x0, blocking collectives: 137 us -> none  [on_device(): lax.all_to_all(outgoing, 'expert', split_axis=0, concat_axis=0, tiled=True)]
    all_to_all x1, waiting for transfers between devices: 125 us -> 25.2 us  [on_device(): lax.all_to_all(send, 'expert', split_axis=0, concat_axis=0, tiled=True, a...]
    ppermute x2 -> x21, starting transfers between devices: 2.86 us -> 59 us  [moved(): return lax.ppermute(block, ('pipe', 'expert'), pairs)]
    ppermute x2 -> x21, waiting for transfers between devices: 21.1 us -> 45.3 us  [moved(): return lax.ppermute(block, ('pipe', 'expert'), pairs)]
    reshape x3 -> x0, local copies, waits for them, and re-layouts: 20 us -> none  [the longest x1 7.26 us: expert_rows(): flat_rows = received.reshape(groups * slots, width)]
    pallas_call x0 -> x3, Pallas kernels: none -> 17.2 us  [the longest x1 11.6 us: expert(): call(expert_kernel, [shape((MAIN, WIDE), BF16)] * CHIPS, [SMEM, VMEM] + [...]
    dot_general x2 -> x0, matrix products: 13.4 us -> none  [the longest x1 8.63 us: expert_rows(): pre = jnp.dot(flat_rows, weights_up, preferred_element_type=jnp.float32)]
    gather x3 -> x0, local copies, waits for them, and re-layouts: 12.3 us -> none  [the longest x1 6.92 us: on_device(): chosen = combined[flat_ids, ranks].reshape(tok_rows, top, width)]
  transfers between devices with their start and end apart: 3 -> 22, of which waited for: 3 -> 7; matrix products, arithmetic and copies ran while one was open for 0% -> 0% of each run, Pallas kernels for 0% -> 0%
where the time goes in v1:
time: 159 us
  waiting for transfers between devices  70.5 us (44%)
  starting transfers between devices  68 us (43%)
  Pallas kernels  17.2 us (11%)
  local copies, waits for them, and re-layouts  2.51 us (2%)
    ppermute x21, starting transfers between devices, moved(): return lax.ppermute(block, ('pipe', 'expert'), pairs)  59 us
    ppermute x21, waiting for transfers between devices, moved(): return lax.ppermute(block, ('pipe', 'expert'), pairs)  45.3 us
    all_to_all x1, waiting for transfers between devices, on_device(): lax.all_to_all(send, 'expert', split_axis=0, concat_axis=0, tiled=True, a...  25.2 us
    pallas_call x1, Pallas kernels, expert(): call(expert_kernel, [shape((MAIN, WIDE), BF16)] * CHIPS, [SMEM, VMEM] + [...  11.6 us
    all_to_all x1, starting transfers between devices, on_device(): lax.all_to_all(send, 'expert', split_axis=0, concat_axis=0, tiled=True, a...  9.01 us
    pallas_call x1, Pallas kernels, build(): call(build_kernel, [pltpu.HBM((CHIPS * MAIN, WIDE), BF16), shape((TOK + M...  4.12 us
  transfers between devices with their start and end apart: 22, of which 7 were waited for; matrix products, arithmetic and copies ran while one was open for 0% of the time, Pallas kernels for 0%

profile of v1, /device:TPU:1, one launch (start us, length us, event | category | flops | bytes accessed | tf_op | source)
XLA Modules:
  0.0 159.0 jit_solution(8175910008221741084)
XLA Ops:
  0.7 0.1 pad_add_fusion.place
  0.7 4.1 %shard_map.86 = (bf16[256,4480]{1,0:T(8,128)(2,1)}, bf16[144,3584]{1,0:T(8,128)(2,1)S(1)}) custom-call(s32[2]{0:T(128)S(1)} %pad_add_fusion.place, bf16[64,3584]{1,0:T(8,128)(2,1)} %bitcast.22, bf16[64,3584]{1,0:T(8,128)(2,1)} %bitcast.23, s32[2,128]{1,0:T(2,128)} %bitcast.26, f32[2,128]{1,0:T(2,128)} %bitcast.27, f32[1,3584]{1,0:T(1,128)} %gain_hbm.1), custom_call_target="tpu_custom_call" | custom-call | tf_op jit(solution)/shard_map/pallas_call | solution.py:112
  4.9 1.0 copy-done
  5.9 3.2 %collective-permute-start.1 = (bf16[3584,1024]{1,0:T(8,128)(2,1)}, bf16[3584,1024]{1,0:T(8,128)(2,1)}, u32[]{:S(2)}, u32[]{:S(2)}) collective-permute-start(bf16[3584,1024]{1,0:T(8,128)(2,1)} %bitcast.17), channel_id=1, source_target_pairs={{0,1},{1,0},{2,3},{3,2},{4,5},{5,4},{6,7},{7,6},{8,9},{9,8},{10,11... | collective-permute-start | bytes 22020104 | tf_op jit(solution)/shard_map/ppermute | solution.py:244
  9.1 9.0 %all-to-all-start = ((bf16[16,16,4480]{2,1,0:T(8,128)(2,1)}), bf16[16,16,4480]{2,1,0:T(8,128)(2,1)S(1)}, u32[]{:S(2)}, u32[]{:S(2)}) async-start(bf16[16,16,4480]{2,1,0:T(8,128)(2,1)} %bitcast.21), calls=%async_computation | async-start | bytes 4587520 | tf_op jit(solution)/shard_map/all_to_all | solution.py:256
  18.1 0.4 collective-permute-start.2
  18.5 2.8 %collective-permute-start = (bf16[144,3584]{1,0:T(8,128)(2,1)}, bf16[144,3584]{1,0:T(8,128)(2,1)S(1)}, u32[]{:S(2)}, u32[]{:S(2)}) collective-permute-start(bf16[144,3584]{1,0:T(8,128)(2,1)} %copy-done), channel_id=1, source_target_pairs={{0,32},{1,225},{2,34},{3,227},{4,36},{5,229},{6,38},{7,231},{8,40}... | collective-permute-start | bytes 3096584 | tf_op jit(solution)/shard_map/ppermute | solution.py:244
  21.2 27.0 %collective-permute-done.carried = bf16[144,3584]{1,0:T(8,128)(2,1)S(1)} collective-permute-done((bf16[144,3584]{1,0:T(8,128)(2,1)}, bf16[144,3584]{1,0:T(8,128)(2,1)S(1)}, u32[]{:S(2)}, u32[]{:S(2)}) %collective-permute-start) | collective-permute-done | bytes 1032224 | tf_op jit(solution)/shard_map/ppermute | solution.py:244
  48.2 0.0 collective-permute-done.2.refs_3_
  48.2 25.2 %all-to-all-done = bf16[16,16,4480]{2,1,0:T(8,128)(2,1)S(1)} async-done(((bf16[16,16,4480]{2,1,0:T(8,128)(2,1)}), bf16[16,16,4480]{2,1,0:T(8,128)(2,1)S(1)}, u32[]{:S(2)}, u32[]{:S(2)}) %all-to-all-start) | async-done | bytes 2293792 | tf_op jit(solution)/shard_map/all_to_all | solution.py:256
  73.4 0.0 collective-permute-done.1.refs_1_
  73.4 11.6 %shard_map.87 = (bf16[16,4480]{1,0:T(8,128)(2,1)S(1)}, bf16[16,4480]{1,0:T(8,128)(2,1)S(1)}, bf16[16,4480]{1,0:T(8,128)(2,1)S(1)}, bf16[16,4480]{1,0:T(8,128)(2,...) custom-call(s32[2]{0:T(128)S(1)} %pad_add_fusion.place, ...), custom_call_target="tpu_custom_call" | custom-call | tf_op jit(solution)/shard_map/pallas_call | solution.py:181
  85.0 2.4 %collective-permute-start.3 = (bf16[16,4480]{1,0:T(8,128)(2,1)S(1)}, bf16[16,4480]{1,0:T(8,128)(2,1)S(1)}, u32[]{:S(2)}, u32[]{:S(2)}) collective-permute-start(bf16[16,4480]{1,0:T(8,128)(2,1)S(1)} %get-tuple-element.40), channel_id=1, source_target_pairs={{0,60},{1,253},{2,62},{3,255},{4,32},{5,225},{6,34},{7,227},{8,36}... | collective-permute-start | bytes 430088 | tf_op jit(solution)/shard_map/ppermute | solution.py:244
  87.4 5.7 %collective-permute-start.4 = (bf16[16,4480]{1,0:T(8,128)(2,1)S(1)}, bf16[16,4480]{1,0:T(8,128)(2,1)S(1)}, u32[]{:S(2)}, u32[]{:S(2)}) collective-permute-start(bf16[16,4480]{1,0:T(8,128)(2,1)S(1)} %get-tuple-element.41), channel_id=1, source_target_pairs={{0,50},{1,243},{2,48},{3,241},{4,54},{5,247},{6,52},{7,245},{8,58}... | collective-permute-start | bytes 430088 | tf_op jit(solution)/shard_map/ppermute | solution.py:244
  93.1 0.3 collective-permute-start.5
  93.4 1.4 collective-permute-start.6
  94.8 2.6 %collective-permute-start.7 = (bf16[16,4480]{1,0:T(8,128)(2,1)S(1)}, bf16[16,4480]{1,0:T(8,128)(2,1)S(1)}, u32[]{:S(2)}, u32[]{:S(2)}) collective-permute-start(bf16[16,4480]{1,0:T(8,128)(2,1)S(1)} %get-tuple-element.44), channel_id=1, source_target_pairs={{0,34},{1,227},{2,32},{3,225},{4,38},{5,231},{6,36},{7,229},{8,42}... | collective-permute-start | bytes 430088 | tf_op jit(solution)/shard_map/ppermute | solution.py:244
  97.4 0.0 collective-permute-done.3.refs_0_
  97.4 1.7 %collective-permute-start.8 = (bf16[16,4480]{1,0:T(8,128)(2,1)S(1)}, bf16[16,4480]{1,0:T(8,128)(2,1)S(1)}, u32[]{:S(2)}, u32[]{:S(2)}) collective-permute-start(bf16[16,4480]{1,0:T(8,128)(2,1)S(1)} %get-tuple-element.45), channel_id=1, source_target_pairs={{0,44},{1,237},{2,46},{3,239},{4,48},{5,241},{6,50},{7,243},{8,52}... | collective-permute-start | bytes 430088 | tf_op jit(solution)/shard_map/ppermute | solution.py:244
  99.1 0.0 collective-permute-done.4.refs_1_
  99.1 7.3 %collective-permute-start.9 = (bf16[16,4480]{1,0:T(8,128)(2,1)S(1)}, bf16[16,4480]{1,0:T(8,128)(2,1)S(1)}, u32[]{:S(2)}, u32[]{:S(2)}) collective-permute-start(bf16[16,4480]{1,0:T(8,128)(2,1)S(1)} %get-tuple-element.46), channel_id=1, source_target_pairs={{0,56},{1,249},{2,58},{3,251},{4,60},{5,253},{6,62},{7,255},{8,32}... | collective-permute-start | bytes 430088 | tf_op jit(solution)/shard_map/ppermute | solution.py:244
  106.4 0.0 collective-permute-done.5.refs_2_
  106.4 3.3 %collective-permute-start.10 = (bf16[16,4480]{1,0:T(8,128)(2,1)S(1)}, bf16[16,4480]{1,0:T(8,128)(2,1)S(1)}, u32[]{:S(2)}, u32[]{:S(2)}) collective-permute-start(bf16[16,4480]{1,0:T(8,128)(2,1)S(1)} %get-tuple-element.47), channel_id=1, source_target_pairs={{0,42},{1,235},{2,40},{3,233},{4,46},{5,239},{6,44},{7,237},{8,50}... | collective-permute-start | bytes 430088 | tf_op jit(solution)/shard_map/ppermute | solution.py:244
  109.7 0.0 collective-permute-done.6.refs_3_
  109.7 2.4 %collective-permute-start.11 = (bf16[16,4480]{1,0:T(8,128)(2,1)S(1)}, bf16[16,4480]{1,0:T(8,128)(2,1)S(1)}, u32[]{:S(2)}, u32[]{:S(2)}) collective-permute-start(bf16[16,4480]{1,0:T(8,128)(2,1)S(1)} %get-tuple-element.48), channel_id=1, source_target_pairs={{0,48},{1,241},{2,50},{3,243},{4,52},{5,245},{6,54},{7,247},{8,56}... | collective-permute-start | bytes 430088 | tf_op jit(solution)/shard_map/ppermute | solution.py:244
  112.1 0.0 collective-permute-done.7.refs_4_
  112.1 5.1 %collective-permute-start.12 = (bf16[16,4480]{1,0:T(8,128)(2,1)S(1)}, bf16[16,4480]{1,0:T(8,128)(2,1)S(1)}, u32[]{:S(2)}, u32[]{:S(2)}) collective-permute-start(bf16[16,4480]{1,0:T(8,128)(2,1)S(1)} %get-tuple-element.49), channel_id=1, source_target_pairs={{0,62},{1,255},{2,60},{3,253},{4,34},{5,227},{6,32},{7,225},{8,38}... | collective-permute-start | bytes 430088 | tf_op jit(solution)/shard_map/ppermute | solution.py:244
  117.3 0.0 collective-permute-done.8.refs_5_
  117.3 0.3 collective-permute-start.13
  117.6 0.0 collective-permute-done.9.refs_6_
  117.6 5.0 %collective-permute-start.14 = (bf16[16,4480]{1,0:T(8,128)(2,1)S(1)}, bf16[16,4480]{1,0:T(8,128)(2,1)S(1)}, u32[]{:S(2)}, u32[]{:S(2)}) collective-permute-start(bf16[16,4480]{1,0:T(8,128)(2,1)S(1)} %get-tuple-element.51), channel_id=1, source_target_pairs={{0,54},{1,247},{2,52},{3,245},{4,58},{5,251},{6,56},{7,249},{8,62}... | collective-permute-start | bytes 430088 | tf_op jit(solution)/shard_map/ppermute | solution.py:244
  122.6 0.0 collective-permute-done.10.refs_7_
  122.6 2.3 %collective-permute-start.15 = (bf16[16,4480]{1,0:T(8,128)(2,1)S(1)}, bf16[16,4480]{1,0:T(8,128)(2,1)S(1)}, u32[]{:S(2)}, u32[]{:S(2)}) collective-permute-start(bf16[16,4480]{1,0:T(8,128)(2,1)S(1)} %get-tuple-element.52), channel_id=1, source_target_pairs={{0,46},{1,239},{2,44},{3,237},{4,50},{5,243},{6,48},{7,241},{8,54}... | collective-permute-start | bytes 430088 | tf_op jit(solution)/shard_map/ppermute | solution.py:244
  124.9 0.1 collective-permute-done.11.refs_8_
  125.0 6.0 %collective-permute-start.16 = (bf16[16,4480]{1,0:T(8,128)(2,1)S(1)}, bf16[16,4480]{1,0:T(8,128)(2,1)S(1)}, u32[]{:S(2)}, u32[]{:S(2)}) collective-permute-start(bf16[16,4480]{1,0:T(8,128)(2,1)S(1)} %get-tuple-element.53), channel_id=1, source_target_pairs={{0,58},{1,251},{2,56},{3,249},{4,62},{5,255},{6,60},{7,253},{8,34}... | collective-permute-start | bytes 430088 | tf_op jit(solution)/shard_map/ppermute | solution.py:244
  131.0 0.0 collective-permute-done.12.refs_9_
  131.0 4.0 %collective-permute-start.18 = (bf16[16,4480]{1,0:T(8,128)(2,1)S(1)}, bf16[16,4480]{1,0:T(8,128)(2,1)S(1)}, u32[]{:S(2)}, u32[]{:S(2)}) collective-permute-start(bf16[16,4480]{1,0:T(8,128)(2,1)S(1)} %get-tuple-element.55), channel_id=1, source_target_pairs={{0,32},{1,225},{2,34},{3,227},{4,36},{5,229},{6,38},{7,231},{8,40}... | collective-permute-start | bytes 430088 | tf_op jit(solution)/shard_map/ppermute | solution.py:244
  135.0 0.0 collective-permute-done.14.refs_11_
  135.0 2.3 %collective-permute-done.15.refs_12_ = bf16[16,4480]{1,0:T(8,128)(2,1)S(1)} collective-permute-done((bf16[16,4480]{1,0:T(8,128)(2,1)S(1)}, bf16[16,4480]{1,0:T(8,128)(2,1)S(1)}, u32[]{:S(2)}, u32[]{:S(2)}) %collective-permute-start.15) | collective-permute-done | bytes 143392 | tf_op jit(solution)/shard_map/ppermute | solution.py:244
  137.3 7.4 %collective-permute-done.16.refs_13_ = bf16[16,4480]{1,0:T(8,128)(2,1)S(1)} collective-permute-done((bf16[16,4480]{1,0:T(8,128)(2,1)S(1)}, bf16[16,4480]{1,0:T(8,128)(2,1)S(1)}, u32[]{:S(2)}, u32[]{:S(2)}) %collective-permute-start.16) | collective-permute-done | bytes 143392 | tf_op jit(solution)/shard_map/ppermute | solution.py:244
  144.7 0.8 collective-permute-done.17.refs_14_
  145.5 1.5 shard_map.88
  147.0 1.9 %collective-permute-start.19 = (bf16[64,3584]{1,0:T(8,128)(2,1)S(1)}, bf16[64,3584]{1,0:T(8,128)(2,1)S(1)}, u32[]{:S(2)}, u32[]{:S(2)}) collective-permute-start(bf16[64,3584]{1,0:T(8,128)(2,1)S(1)} %get-tuple-element.56), channel_id=1, source_target_pairs={{0,0},{1,65},{2,2},{3,67},{4,4},{5,69},{6,6},{7,71},{8,8},{9,73},{... | collective-permute-start | bytes 1376264 | tf_op jit(solution)/shard_map/ppermute | solution.py:244
  148.9 0.7 collective-permute-start.20
  149.6 7.8 %collective-permute-done.19 = bf16[64,3584]{1,0:T(8,128)(2,1)S(1)} collective-permute-done((bf16[64,3584]{1,0:T(8,128)(2,1)S(1)}, bf16[64,3584]{1,0:T(8,128)(2,1)S(1)}, u32[]{:S(2)}, u32[]{:S(2)}) %collective-permute-start.19) | collective-permute-done | bytes 458784 | tf_op jit(solution)/shard_map/ppermute | solution.py:244
  157.4 0.0 collective-permute-done.20
  157.4 0.8 copy.11
  158.2 0.8 copy.12
  (4 shorter events, 0.0 us)
Async XLA Ops:
  4.9 1.0 copy-start
  5.9 67.5 %collective-permute-start.1 = (bf16[3584,1024]{1,0:T(8,128)(2,1)}, bf16[3584,1024]{1,0:T(8,128)(2,1)}, u32[]{:S(2)}, u32[]{:S(2)}) collective-permute-start(bf16[3584,1024]{1,0:T(8,128)(2,1)} %bitcast.17), channel_id=1, source_target_pairs={{0,1},{1,0},{2,3},{3,2},{4,5},{5,4},{6,7},{7,6},{8,9},{9,8},{10,11... | collective-permute-start | bytes 22020104 | tf_op jit(solution)/shard_map/ppermute | solution.py:244
  9.1 64.3 %all-to-all-start = ((bf16[16,16,4480]{2,1,0:T(8,128)(2,1)}), bf16[16,16,4480]{2,1,0:T(8,128)(2,1)S(1)}, u32[]{:S(2)}, u32[]{:S(2)}) async-start(bf16[16,16,4480]{2,1,0:T(8,128)(2,1)} %bitcast.21), calls=%async_computation | async-start | bytes 4587520 | tf_op jit(solution)/shard_map/all_to_all | solution.py:256
  18.1 30.1 %collective-permute-start.2 = (bf16[512,3584]{1,0:T(8,128)(2,1)}, bf16[512,3584]{1,0:T(8,128)(2,1)}, u32[]{:S(2)}, u32[]{:S(2)}) collective-permute-start(bf16[512,3584]{1,0:T(8,128)(2,1)} %bitcast.19), channel_id=1, source_target_pairs={{0,1},{1,0},{2,3},{3,2},{4,5},{5,4},{6,7},{7,6},{8,9},{9,8},{10,11... | collective-permute-start | bytes 11010056 | tf_op jit(solution)/shard_map/ppermute | solution.py:244
  18.5 29.7 %collective-permute-start = (bf16[144,3584]{1,0:T(8,128)(2,1)}, bf16[144,3584]{1,0:T(8,128)(2,1)S(1)}, u32[]{:S(2)}, u32[]{:S(2)}) collective-permute-start(bf16[144,3584]{1,0:T(8,128)(2,1)} %copy-done), channel_id=1, source_target_pairs={{0,32},{1,225},{2,34},{3,227},{4,36},{5,229},{6,38},{7,231},{8,40}... | collective-permute-start | bytes 3096584 | tf_op jit(solution)/shard_map/ppermute | solution.py:244
  85.0 12.4 %collective-permute-start.3 = (bf16[16,4480]{1,0:T(8,128)(2,1)S(1)}, bf16[16,4480]{1,0:T(8,128)(2,1)S(1)}, u32[]{:S(2)}, u32[]{:S(2)}) collective-permute-start(bf16[16,4480]{1,0:T(8,128)(2,1)S(1)} %get-tuple-element.40), channel_id=1, source_target_pairs={{0,60},{1,253},{2,62},{3,255},{4,32},{5,225},{6,34},{7,227},{8,36}... | collective-permute-start | bytes 430088 | tf_op jit(solution)/shard_map/ppermute | solution.py:244
  87.4 11.7 %collective-permute-start.4 = (bf16[16,4480]{1,0:T(8,128)(2,1)S(1)}, bf16[16,4480]{1,0:T(8,128)(2,1)S(1)}, u32[]{:S(2)}, u32[]{:S(2)}) collective-permute-start(bf16[16,4480]{1,0:T(8,128)(2,1)S(1)} %get-tuple-element.41), channel_id=1, source_target_pairs={{0,50},{1,243},{2,48},{3,241},{4,54},{5,247},{6,52},{7,245},{8,58}... | collective-permute-start | bytes 430088 | tf_op jit(solution)/shard_map/ppermute | solution.py:244
  93.1 13.3 %collective-permute-start.5 = (bf16[16,4480]{1,0:T(8,128)(2,1)S(1)}, bf16[16,4480]{1,0:T(8,128)(2,1)S(1)}, u32[]{:S(2)}, u32[]{:S(2)}) collective-permute-start(bf16[16,4480]{1,0:T(8,128)(2,1)S(1)} %get-tuple-element.42), channel_id=1, source_target_pairs={{0,36},{1,229},{2,38},{3,231},{4,40},{5,233},{6,42},{7,235},{8,44}... | collective-permute-start | bytes 430088 | tf_op jit(solution)/shard_map/ppermute | solution.py:244
  93.4 16.3 %collective-permute-start.6 = (bf16[16,4480]{1,0:T(8,128)(2,1)S(1)}, bf16[16,4480]{1,0:T(8,128)(2,1)S(1)}, u32[]{:S(2)}, u32[]{:S(2)}) collective-permute-start(bf16[16,4480]{1,0:T(8,128)(2,1)S(1)} %get-tuple-element.43), channel_id=1, source_target_pairs={{0,52},{1,245},{2,54},{3,247},{4,56},{5,249},{6,58},{7,251},{8,60}... | collective-permute-start | bytes 430088 | tf_op jit(solution)/shard_map/ppermute | solution.py:244
  94.8 17.3 %collective-permute-start.7 = (bf16[16,4480]{1,0:T(8,128)(2,1)S(1)}, bf16[16,4480]{1,0:T(8,128)(2,1)S(1)}, u32[]{:S(2)}, u32[]{:S(2)}) collective-permute-start(bf16[16,4480]{1,0:T(8,128)(2,1)S(1)} %get-tuple-element.44), channel_id=1, source_target_pairs={{0,34},{1,227},{2,32},{3,225},{4,38},{5,231},{6,36},{7,229},{8,42}... | collective-permute-start | bytes 430088 | tf_op jit(solution)/shard_map/ppermute | solution.py:244
  97.4 19.9 %collective-permute-start.8 = (bf16[16,4480]{1,0:T(8,128)(2,1)S(1)}, bf16[16,4480]{1,0:T(8,128)(2,1)S(1)}, u32[]{:S(2)}, u32[]{:S(2)}) collective-permute-start(bf16[16,4480]{1,0:T(8,128)(2,1)S(1)} %get-tuple-element.45), channel_id=1, source_target_pairs={{0,44},{1,237},{2,46},{3,239},{4,48},{5,241},{6,50},{7,243},{8,52}... | collective-permute-start | bytes 430088 | tf_op jit(solution)/shard_map/ppermute | solution.py:244
  99.1 18.5 %collective-permute-start.9 = (bf16[16,4480]{1,0:T(8,128)(2,1)S(1)}, bf16[16,4480]{1,0:T(8,128)(2,1)S(1)}, u32[]{:S(2)}, u32[]{:S(2)}) collective-permute-start(bf16[16,4480]{1,0:T(8,128)(2,1)S(1)} %get-tuple-element.46), channel_id=1, source_target_pairs={{0,56},{1,249},{2,58},{3,251},{4,60},{5,253},{6,62},{7,255},{8,32}... | collective-permute-start | bytes 430088 | tf_op jit(solution)/shard_map/ppermute | solution.py:244
  106.4 16.2 %collective-permute-start.10 = (bf16[16,4480]{1,0:T(8,128)(2,1)S(1)}, bf16[16,4480]{1,0:T(8,128)(2,1)S(1)}, u32[]{:S(2)}, u32[]{:S(2)}) collective-permute-start(bf16[16,4480]{1,0:T(8,128)(2,1)S(1)} %get-tuple-element.47), channel_id=1, source_target_pairs={{0,42},{1,235},{2,40},{3,233},{4,46},{5,239},{6,44},{7,237},{8,50}... | collective-permute-start | bytes 430088 | tf_op jit(solution)/shard_map/ppermute | solution.py:244
  109.7 15.2 %collective-permute-start.11 = (bf16[16,4480]{1,0:T(8,128)(2,1)S(1)}, bf16[16,4480]{1,0:T(8,128)(2,1)S(1)}, u32[]{:S(2)}, u32[]{:S(2)}) collective-permute-start(bf16[16,4480]{1,0:T(8,128)(2,1)S(1)} %get-tuple-element.48), channel_id=1, source_target_pairs={{0,48},{1,241},{2,50},{3,243},{4,52},{5,245},{6,54},{7,247},{8,56}... | collective-permute-start | bytes 430088 | tf_op jit(solution)/shard_map/ppermute | solution.py:244
  112.1 18.9 %collective-permute-start.12 = (bf16[16,4480]{1,0:T(8,128)(2,1)S(1)}, bf16[16,4480]{1,0:T(8,128)(2,1)S(1)}, u32[]{:S(2)}, u32[]{:S(2)}) collective-permute-start(bf16[16,4480]{1,0:T(8,128)(2,1)S(1)} %get-tuple-element.49), channel_id=1, source_target_pairs={{0,62},{1,255},{2,60},{3,253},{4,34},{5,227},{6,32},{7,225},{8,38}... | collective-permute-start | bytes 430088 | tf_op jit(solution)/shard_map/ppermute | solution.py:244
  117.3 13.7 %collective-permute-start.13 = (bf16[16,4480]{1,0:T(8,128)(2,1)S(1)}, bf16[16,4480]{1,0:T(8,128)(2,1)S(1)}, u32[]{:S(2)}, u32[]{:S(2)}) collective-permute-start(bf16[16,4480]{1,0:T(8,128)(2,1)S(1)} %get-tuple-element.50), channel_id=1, source_target_pairs={{0,38},{1,231},{2,36},{3,229},{4,42},{5,235},{6,40},{7,233},{8,46}... | collective-permute-start | bytes 430088 | tf_op jit(solution)/shard_map/ppermute | solution.py:244
  117.6 17.5 %collective-permute-start.14 = (bf16[16,4480]{1,0:T(8,128)(2,1)S(1)}, bf16[16,4480]{1,0:T(8,128)(2,1)S(1)}, u32[]{:S(2)}, u32[]{:S(2)}) collective-permute-start(bf16[16,4480]{1,0:T(8,128)(2,1)S(1)} %get-tuple-element.51), channel_id=1, source_target_pairs={{0,54},{1,247},{2,52},{3,245},{4,58},{5,251},{6,56},{7,249},{8,62}... | collective-permute-start | bytes 430088 | tf_op jit(solution)/shard_map/ppermute | solution.py:244
  122.6 14.7 %collective-permute-start.15 = (bf16[16,4480]{1,0:T(8,128)(2,1)S(1)}, bf16[16,4480]{1,0:T(8,128)(2,1)S(1)}, u32[]{:S(2)}, u32[]{:S(2)}) collective-permute-start(bf16[16,4480]{1,0:T(8,128)(2,1)S(1)} %get-tuple-element.52), channel_id=1, source_target_pairs={{0,46},{1,239},{2,44},{3,237},{4,50},{5,243},{6,48},{7,241},{8,54}... | collective-permute-start | bytes 430088 | tf_op jit(solution)/shard_map/ppermute | solution.py:244
  125.0 19.8 %collective-permute-start.16 = (bf16[16,4480]{1,0:T(8,128)(2,1)S(1)}, bf16[16,4480]{1,0:T(8,128)(2,1)S(1)}, u32[]{:S(2)}, u32[]{:S(2)}) collective-permute-start(bf16[16,4480]{1,0:T(8,128)(2,1)S(1)} %get-tuple-element.53), channel_id=1, source_target_pairs={{0,58},{1,251},{2,56},{3,249},{4,62},{5,255},{6,60},{7,253},{8,34}... | collective-permute-start | bytes 430088 | tf_op jit(solution)/shard_map/ppermute | solution.py:244
  131.0 14.5 %collective-permute-start.17 = (bf16[16,4480]{1,0:T(8,128)(2,1)S(1)}, bf16[16,4480]{1,0:T(8,128)(2,1)S(1)}, u32[]{:S(2)}, u32[]{:S(2)}) collective-permute-start(bf16[16,4480]{1,0:T(8,128)(2,1)S(1)} %get-tuple-element.54), channel_id=1, source_target_pairs={{0,40},{1,233},{2,42},{3,235},{4,44},{5,237},{6,46},{7,239},{8,48}... | collective-permute-start | bytes 430088 | tf_op jit(solution)/shard_map/ppermute | solution.py:244
  131.0 14.5 %collective-permute-start.18 = (bf16[16,4480]{1,0:T(8,128)(2,1)S(1)}, bf16[16,4480]{1,0:T(8,128)(2,1)S(1)}, u32[]{:S(2)}, u32[]{:S(2)}) collective-permute-start(bf16[16,4480]{1,0:T(8,128)(2,1)S(1)} %get-tuple-element.55), channel_id=1, source_target_pairs={{0,32},{1,225},{2,34},{3,227},{4,36},{5,229},{6,38},{7,231},{8,40}... | collective-permute-start | bytes 430088 | tf_op jit(solution)/shard_map/ppermute | solution.py:244
  147.0 10.4 %collective-permute-start.19 = (bf16[64,3584]{1,0:T(8,128)(2,1)S(1)}, bf16[64,3584]{1,0:T(8,128)(2,1)S(1)}, u32[]{:S(2)}, u32[]{:S(2)}) collective-permute-start(bf16[64,3584]{1,0:T(8,128)(2,1)S(1)} %get-tuple-element.56), channel_id=1, source_target_pairs={{0,0},{1,65},{2,2},{3,67},{4,4},{5,69},{6,6},{7,71},{8,8},{9,73},{... | collective-permute-start | bytes 1376264 | tf_op jit(solution)/shard_map/ppermute | solution.py:244
  148.9 8.5 %collective-permute-start.20 = (bf16[64,3584]{1,0:T(8,128)(2,1)S(1)}, bf16[64,3584]{1,0:T(8,128)(2,1)S(1)}, u32[]{:S(2)}, u32[]{:S(2)}) collective-permute-start(bf16[64,3584]{1,0:T(8,128)(2,1)S(1)} %get-tuple-element.57), channel_id=1, source_target_pairs={{0,192},{1,1},{2,194},{3,3},{4,196},{5,5},{6,198},{7,7},{8,200},{9... | collective-permute-start | bytes 1376264 | tf_op jit(solution)/shard_map/ppermute | solution.py:244

commit v2 on v1

--- a/solution.py
+++ b/solution.py
@@ -41,7 +41,7 @@
 
 
 def build_kernel(place, fwd, bwd, ids_hbm, weights_hbm, gain_hbm, *refs):
-    send, carried, ids, weights, gain, packed, sems = refs
+    send, beside, carried, ids, weights, gain, packed, sems = refs
     loads = [
         pltpu.make_async_copy(source, target, sems.at[at])
         for at, (source, target) in enumerate(
@@ -82,7 +82,8 @@
     values = carried[0:TOK, :].astype(F32)
     scale = lax.rsqrt(jnp.mean(values * values, axis=-1, keepdims=True) + 1e-06)
     normed = (values * scale * gain[...]).astype(BF16)
-    stores = []
+    stores = [pltpu.make_async_copy(carried, beside, sems.at[10])]
+    stores[0].start()
     extra = jnp.zeros((CHIPS * MAIN, QUART), F32)
     for j in range(5):
         cols = slice(j * QUART, (j + 1) * QUART)
@@ -108,18 +109,18 @@
 
 
 def build(place, *arrays):
-    shape = jax.ShapeDtypeStruct
     return call(
         build_kernel,
-        [pltpu.HBM((CHIPS * MAIN, WIDE), BF16), shape((TOK + META, D), BF16)],
+        [pltpu.HBM((CHIPS * MAIN, WIDE), BF16), pltpu.HBM((TOK + META, D), BF16)],
         [SMEM] + [HBM] * 5,
-        [HBM, VMEM],
+        [HBM] * 2,
         [
+            pltpu.VMEM((TOK + META, D), BF16),
             pltpu.VMEM((2, TOK), jnp.int32),
             pltpu.VMEM((2, TOK), F32),
             pltpu.VMEM((1, D), F32),
             pltpu.VMEM((CHIPS * MAIN, WIDE), BF16),
-            pltpu.SemaphoreType.DMA((10,)),
+            pltpu.SemaphoreType.DMA((11,)),
         ],
     )(place, *(pltpu.with_memory_space_constraint(a, pltpu.HBM) for a in arrays))
 
@@ -195,12 +196,12 @@
     )(place, recv, *(pltpu.with_memory_space_constraint(w, pltpu.HBM) for w in (*ups, *downs)))
 
 
-def combine_kernel(carried, *refs):
-    blocks, outs, main_all, rest_all = refs[:CHIPS], refs[CHIPS : CHIPS + 2], refs[CHIPS + 2], refs[CHIPS + 3]
-    meta = carried[TOK : TOK + META, 0:TOK].astype(F32)
+def summed(at, carried, blocks, main_all, rest_all, out):
+    take = (iota((TOK, HALF), 0) == iota((TOK, HALF), 1) + at).astype(BF16)
+    meta = jnp.dot(carried[TOK : TOK + META, 0:TOK], take, preferred_element_type=F32)
     numbers = [meta[k : k + 1, :].astype(jnp.int32) for k in range(2)]
     ranks = [meta[2 + k : 3 + k, :].astype(jnp.int32) for k in range(2)]
-    main, rest = slot_masks(numbers, ranks, TOK)
+    main, rest = slot_masks(numbers, ranks, HALF)
     for i in range(CHIPS):
         main_all[i * MAIN : (i + 1) * MAIN, :] = blocks[i][:, 0:D]
         rest_all[i * MAIN : (i + 1) * MAIN, :] = blocks[i][:, D:WIDE]
@@ -220,19 +221,57 @@
     for j in range(4):
         cols = slice(j * QUART, (j + 1) * QUART)
         mixed = product(main_w, main_all[:, cols]) + product(weighed(rest[j]), rest_all[...])
-        updated = (carried[0:TOK, cols].astype(F32) + mixed).astype(BF16)
-        outs[0][:, cols] = updated[0:HALF]
-        outs[1][:, cols] = updated[HALF:TOK]
-
-
-def combine(carried, blocks):
-    return call(
-        combine_kernel,
-        [jax.ShapeDtypeStruct((HALF, D), BF16)] * 2,
-        [VMEM] * (CHIPS + 1),
-        [VMEM] * 2,
-        [pltpu.VMEM((CHIPS * MAIN, D), BF16), pltpu.VMEM((CHIPS * MAIN, QUART), BF16)],
-    )(carried, *blocks)
+        out[:, cols] = (carried[pl.ds(at, HALF), cols].astype(F32) + mixed).astype(BF16)
+
+
+def going_kernel(core, carried, *refs):
+    at = pl.multiple_of(HALF * (1 - core[0]), HALF)
+    summed(at, carried, refs[:CHIPS], refs[CHIPS + 1], refs[CHIPS + 2], refs[CHIPS])
+
+
+def stored(core, rows, targets, sem):
+    for c in range(2):
+
+        @pl.when(core[0] == c)
+        def _():
+            copy = pltpu.make_async_copy(rows, targets[c], sem)
+            copy.start()
+            copy.wait()
+
+
+def staying_kernel(core, carried, *refs):
+    blocks, (fwd, bwd, main_all, rest_all, rows, sem) = refs[:CHIPS], refs[CHIPS:]
+    summed(pl.multiple_of(HALF * core[0], HALF), carried, blocks, main_all, rest_all, rows)
+    stored(core, rows, (fwd, bwd), sem)
+
+
+def came_kernel(core, came, fwd_held, bwd_held, fwd, bwd, sem):
+    stored(core, came, (bwd, fwd), sem)
+
+
+def going(core, carried, blocks):
+    scratch = [pltpu.VMEM((CHIPS * MAIN, D), BF16), pltpu.VMEM((CHIPS * MAIN, QUART), BF16)]
+    out = jax.ShapeDtypeStruct((HALF, D), BF16)
+    return call(going_kernel, out, [SMEM] + [VMEM] * (CHIPS + 1), VMEM, scratch)(core, carried, *blocks)
+
+
+def staying(core, carried, blocks):
+    scratch = [pltpu.VMEM((CHIPS * MAIN, D), BF16), pltpu.VMEM((CHIPS * MAIN, QUART), BF16)]
+    scratch += [pltpu.VMEM((HALF, D), BF16), pltpu.SemaphoreType.DMA]
+    out = [pltpu.HBM((HALF, D), BF16)] * 2
+    return call(staying_kernel, out, [SMEM] + [VMEM] * (CHIPS + 1), [HBM] * 2, scratch)(core, carried, *blocks)
+
+
+def arrive(core, came, fwd, bwd):
+    return pl.pallas_call(
+        came_kernel,
+        out_shape=[pltpu.HBM((HALF, D), BF16)] * 2,
+        in_specs=[SMEM, VMEM, HBM, HBM],
+        out_specs=[HBM] * 2,
+        scratch_shapes=[pltpu.SemaphoreType.DMA],
+        input_output_aliases={2: 0, 3: 1},
+        compiler_params=pltpu.CompilerParams(vmem_limit_bytes=4 * 2**20),
+    )(core, came, fwd, bwd)
 
 
 def moved(block, route):
@@ -260,9 +299,9 @@
     back = []
     for (dz, dx), block in zip(ORDER, expert(place, recv, ups, downs)):
         back.append(moved(block, lambda p, z, xh, c, dz=dz, dx=dx: (p + 1 - 2 * c, z - dz, xh + dx, c)))
-    fwd, bwd = combine(beside, back)
-    fwd_next = moved(fwd, lambda p, z, xh, c: (p + 2 * c, z, xh, c))
-    bwd_next = moved(bwd, lambda p, z, xh, c: (p - 2 + 2 * c, z, xh, c))
+    core = (spot % 2).astype(jnp.int32).reshape(1)
+    came = moved(going(core, beside, back), lambda p, z, xh, c: (p - 2 + 4 * c, z, xh, c))
+    fwd_next, bwd_next = arrive(core, came, *staying(core, beside, back))
     return fwd_next[None], bwd_next[None]
 
 

time: 159 us -> 157 us (0.987)
  Pallas kernels: 17.2 us -> 21.2 us
  local copies, waits for them, and re-layouts: 2.51 us -> 0 us
  waiting for transfers between devices: 70.5 us -> 68 us
  starting transfers between devices: 68 us -> 65.6 us
    pallas_call x2 -> x4, Pallas kernels: 5.64 us -> 8.87 us  [the longest x1 4.08 us: build(): call(build_kernel, [pltpu.HBM((CHIPS * MAIN, WIDE), BF16), pltpu.HBM((TOK...]
    ppermute x21 -> x20, waiting for transfers between devices: 45.3 us -> 42.7 us  [moved(): return lax.ppermute(block, ('pipe', 'expert'), pairs)]
    unnamed x4 -> x0, local copies, waits for them, and re-layouts: 2.51 us -> none
    ppermute x21 -> x20, starting transfers between devices: 59 us -> 56.6 us  [moved(): return lax.ppermute(block, ('pipe', 'expert'), pairs)]
  transfers between devices with their start and end apart: 22 -> 21, of which waited for: 7 -> 5; matrix products, arithmetic and copies ran while one was open for 0% -> 0% of each run, Pallas kernels for 0% -> 2%
where the time goes in v2:
time: 157 us; the launch traced here: 156 us
  waiting for transfers between devices  68 us (43%)
  starting transfers between devices  65.6 us (42%)
  Pallas kernels  21.2 us (14%)
    ppermute x20, starting transfers between devices, moved(): return lax.ppermute(block, ('pipe', 'expert'), pairs)  56.6 us
    ppermute x20, waiting for transfers between devices, moved(): return lax.ppermute(block, ('pipe', 'expert'), pairs)  42.7 us
    all_to_all x1, waiting for transfers between devices, on_device(): lax.all_to_all(send, 'expert', split_axis=0, concat_axis=0, tiled=True, a...  25.3 us
    pallas_call x1, Pallas kernels, expert(): call(expert_kernel, [shape((MAIN, WIDE), BF16)] * CHIPS, [SMEM, VMEM] + [...  12.3 us
    all_to_all x1, starting transfers between devices, on_device(): lax.all_to_all(send, 'expert', split_axis=0, concat_axis=0, tiled=True, a...  9.01 us
    pallas_call x1, Pallas kernels, build(): call(build_kernel, [pltpu.HBM((CHIPS * MAIN, WIDE), BF16), pltpu.HBM((TOK...  4.08 us
  transfers between devices with their start and end apart: 21, of which 5 were waited for; matrix products, arithmetic and copies ran while one was open for 0% of the time, Pallas kernels for 2%

profile of v2, /device:TPU:1, one launch (start us, length us, event | category | flops | bytes accessed | tf_op | source)
XLA Modules:
  0.0 155.7 jit_solution(14266319518678168365)
XLA Ops:
  0.7 0.1 pad_add_fusion.place
  0.7 4.1 %shard_map.86 = (bf16[256,4480]{1,0:T(8,128)(2,1)}, bf16[144,3584]{1,0:T(8,128)(2,1)}) custom-call(s32[2]{0:T(128)S(1)} %pad_add_fusion.place, bf16[64,3584]{1,0:T(8,128)(2,1)} %bitcast.23, bf16[64,3584]{1,0:T(8,128)(2,1)} %bitcast.24, s32[2,128]{1,0:T(2,128)} %bitcast.27, f32[2,128]{1,0:T(2,128)} %bitcast.28, f32[1,3584]{1,0:T(1,128)} %gain_hbm.1), custom_call_target="tpu_custom_call" | custom-call | tf_op jit(solution)/shard_map/pallas_call | solution.py:112
  4.8 3.3 %collective-permute-start.1 = (bf16[3584,1024]{1,0:T(8,128)(2,1)}, bf16[3584,1024]{1,0:T(8,128)(2,1)}, u32[]{:S(2)}, u32[]{:S(2)}) collective-permute-start(bf16[3584,1024]{1,0:T(8,128)(2,1)} %bitcast.18), channel_id=1, source_target_pairs={{0,1},{1,0},{2,3},{3,2},{4,5},{5,4},{6,7},{7,6},{8,9},{9,8},{10,11... | collective-permute-start | bytes 22020104 | tf_op jit(solution)/shard_map/ppermute | solution.py:283
  8.2 9.0 %all-to-all-start = ((bf16[16,16,4480]{2,1,0:T(8,128)(2,1)}), bf16[16,16,4480]{2,1,0:T(8,128)(2,1)S(1)}, u32[]{:S(2)}, u32[]{:S(2)}) async-start(bf16[16,16,4480]{2,1,0:T(8,128)(2,1)} %bitcast.22), calls=%async_computation | async-start | bytes 4587520 | tf_op jit(solution)/shard_map/all_to_all | solution.py:295
  17.2 0.4 collective-permute-start.2
  17.6 2.8 %collective-permute-start = (bf16[144,3584]{1,0:T(8,128)(2,1)}, bf16[144,3584]{1,0:T(8,128)(2,1)S(1)}, u32[]{:S(2)}, u32[]{:S(2)}) collective-permute-start(bf16[144,3584]{1,0:T(8,128)(2,1)} %get-tuple-element.33), channel_id=1, source_target_pairs={{0,32},{1,225},{2,34},{3,227},{4,36},{5,229},{6,38},{7,231},{8,40}... | collective-permute-start | bytes 3096584 | tf_op jit(solution)/shard_map/ppermute | solution.py:283
  20.3 26.9 %collective-permute-done.carried = bf16[144,3584]{1,0:T(8,128)(2,1)S(1)} collective-permute-done((bf16[144,3584]{1,0:T(8,128)(2,1)}, bf16[144,3584]{1,0:T(8,128)(2,1)S(1)}, u32[]{:S(2)}, u32[]{:S(2)}) %collective-permute-start) | collective-permute-done | bytes 1032224 | tf_op jit(solution)/shard_map/ppermute | solution.py:283
  47.3 0.0 collective-permute-done.2.refs_3_
  47.3 25.3 %all-to-all-done = bf16[16,16,4480]{2,1,0:T(8,128)(2,1)S(1)} async-done(((bf16[16,16,4480]{2,1,0:T(8,128)(2,1)}), bf16[16,16,4480]{2,1,0:T(8,128)(2,1)S(1)}, u32[]{:S(2)}, u32[]{:S(2)}) %all-to-all-start) | async-done | bytes 2293792 | tf_op jit(solution)/shard_map/all_to_all | solution.py:295
  72.5 0.0 collective-permute-done.1.refs_1_
  72.5 12.3 %shard_map.87 = (bf16[16,4480]{1,0:T(8,128)(2,1)S(1)}, bf16[16,4480]{1,0:T(8,128)(2,1)S(1)}, bf16[16,4480]{1,0:T(8,128)(2,1)S(1)}, bf16[16,4480]{1,0:T(8,128)(2,...) custom-call(s32[2]{0:T(128)S(1)} %pad_add_fusion.place, ...), custom_call_target="tpu_custom_call" | custom-call | tf_op jit(solution)/shard_map/pallas_call | solution.py:182
  84.9 2.3 %collective-permute-start.3 = (bf16[16,4480]{1,0:T(8,128)(2,1)S(1)}, bf16[16,4480]{1,0:T(8,128)(2,1)S(1)}, u32[]{:S(2)}, u32[]{:S(2)}) collective-permute-start(bf16[16,4480]{1,0:T(8,128)(2,1)S(1)} %get-tuple-element.42), channel_id=1, source_target_pairs={{0,60},{1,253},{2,62},{3,255},{4,32},{5,225},{6,34},{7,227},{8,36}... | collective-permute-start | bytes 430088 | tf_op jit(solution)/shard_map/ppermute | solution.py:283
  87.2 5.7 %collective-permute-start.4 = (bf16[16,4480]{1,0:T(8,128)(2,1)S(1)}, bf16[16,4480]{1,0:T(8,128)(2,1)S(1)}, u32[]{:S(2)}, u32[]{:S(2)}) collective-permute-start(bf16[16,4480]{1,0:T(8,128)(2,1)S(1)} %get-tuple-element.43), channel_id=1, source_target_pairs={{0,50},{1,243},{2,48},{3,241},{4,54},{5,247},{6,52},{7,245},{8,58}... | collective-permute-start | bytes 430088 | tf_op jit(solution)/shard_map/ppermute | solution.py:283
  92.9 0.1 collective-permute-start.5
  93.0 1.6 %collective-permute-start.6 = (bf16[16,4480]{1,0:T(8,128)(2,1)S(1)}, bf16[16,4480]{1,0:T(8,128)(2,1)S(1)}, u32[]{:S(2)}, u32[]{:S(2)}) collective-permute-start(bf16[16,4480]{1,0:T(8,128)(2,1)S(1)} %get-tuple-element.45), channel_id=1, source_target_pairs={{0,52},{1,245},{2,54},{3,247},{4,56},{5,249},{6,58},{7,251},{8,60}... | collective-permute-start | bytes 430088 | tf_op jit(solution)/shard_map/ppermute | solution.py:283
  94.6 2.6 %collective-permute-start.7 = (bf16[16,4480]{1,0:T(8,128)(2,1)S(1)}, bf16[16,4480]{1,0:T(8,128)(2,1)S(1)}, u32[]{:S(2)}, u32[]{:S(2)}) collective-permute-start(bf16[16,4480]{1,0:T(8,128)(2,1)S(1)} %get-tuple-element.46), channel_id=1, source_target_pairs={{0,34},{1,227},{2,32},{3,225},{4,38},{5,231},{6,36},{7,229},{8,42}... | collective-permute-start | bytes 430088 | tf_op jit(solution)/shard_map/ppermute | solution.py:283
  97.2 0.0 collective-permute-done.3.refs_0_
  97.2 6.1 %collective-permute-start.8 = (bf16[16,4480]{1,0:T(8,128)(2,1)S(1)}, bf16[16,4480]{1,0:T(8,128)(2,1)S(1)}, u32[]{:S(2)}, u32[]{:S(2)}) collective-permute-start(bf16[16,4480]{1,0:T(8,128)(2,1)S(1)} %get-tuple-element.47), channel_id=1, source_target_pairs={{0,44},{1,237},{2,46},{3,239},{4,48},{5,241},{6,50},{7,243},{8,52}... | collective-permute-start | bytes 430088 | tf_op jit(solution)/shard_map/ppermute | solution.py:283
  103.3 0.0 collective-permute-done.4.refs_1_
  103.3 2.7 %collective-permute-start.9 = (bf16[16,4480]{1,0:T(8,128)(2,1)S(1)}, bf16[16,4480]{1,0:T(8,128)(2,1)S(1)}, u32[]{:S(2)}, u32[]{:S(2)}) collective-permute-start(bf16[16,4480]{1,0:T(8,128)(2,1)S(1)} %get-tuple-element.48), channel_id=1, source_target_pairs={{0,56},{1,249},{2,58},{3,251},{4,60},{5,253},{6,62},{7,255},{8,32}... | collective-permute-start | bytes 430088 | tf_op jit(solution)/shard_map/ppermute | solution.py:283
  106.1 0.0 collective-permute-done.5.refs_2_
  106.1 3.5 %collective-permute-start.10 = (bf16[16,4480]{1,0:T(8,128)(2,1)S(1)}, bf16[16,4480]{1,0:T(8,128)(2,1)S(1)}, u32[]{:S(2)}, u32[]{:S(2)}) collective-permute-start(bf16[16,4480]{1,0:T(8,128)(2,1)S(1)} %get-tuple-element.49), channel_id=1, source_target_pairs={{0,42},{1,235},{2,40},{3,233},{4,46},{5,239},{6,44},{7,237},{8,50}... | collective-permute-start | bytes 430088 | tf_op jit(solution)/shard_map/ppermute | solution.py:283
  109.6 0.0 collective-permute-done.6.refs_3_
  109.6 2.6 %collective-permute-start.11 = (bf16[16,4480]{1,0:T(8,128)(2,1)S(1)}, bf16[16,4480]{1,0:T(8,128)(2,1)S(1)}, u32[]{:S(2)}, u32[]{:S(2)}) collective-permute-start(bf16[16,4480]{1,0:T(8,128)(2,1)S(1)} %get-tuple-element.50), channel_id=1, source_target_pairs={{0,48},{1,241},{2,50},{3,243},{4,52},{5,245},{6,54},{7,247},{8,56}... | collective-permute-start | bytes 430088 | tf_op jit(solution)/shard_map/ppermute | solution.py:283
  112.2 0.0 collective-permute-done.7.refs_4_
  112.2 6.1 %collective-permute-start.12 = (bf16[16,4480]{1,0:T(8,128)(2,1)S(1)}, bf16[16,4480]{1,0:T(8,128)(2,1)S(1)}, u32[]{:S(2)}, u32[]{:S(2)}) collective-permute-start(bf16[16,4480]{1,0:T(8,128)(2,1)S(1)} %get-tuple-element.51), channel_id=1, source_target_pairs={{0,62},{1,255},{2,60},{3,253},{4,34},{5,227},{6,32},{7,225},{8,38}... | collective-permute-start | bytes 430088 | tf_op jit(solution)/shard_map/ppermute | solution.py:283
  118.3 0.0 collective-permute-done.8.refs_5_
  118.3 0.0 collective-permute-start.13
  118.3 0.0 collective-permute-done.9.refs_6_
  118.3 3.4 %collective-permute-start.14 = (bf16[16,4480]{1,0:T(8,128)(2,1)}, bf16[16,4480]{1,0:T(8,128)(2,1)S(1)}, u32[]{:S(2)}, u32[]{:S(2)}) collective-permute-start(bf16[16,4480]{1,0:T(8,128)(2,1)} %get-tuple-element.53), channel_id=1, source_target_pairs={{0,54},{1,247},{2,52},{3,245},{4,58},{5,251},{6,56},{7,249},{8,62}... | collective-permute-start | bytes 430088 | tf_op jit(solution)/shard_map/ppermute | solution.py:283
  121.7 0.0 collective-permute-done.10.refs_7_
  121.7 2.7 %collective-permute-start.15 = (bf16[16,4480]{1,0:T(8,128)(2,1)}, bf16[16,4480]{1,0:T(8,128)(2,1)S(1)}, u32[]{:S(2)}, u32[]{:S(2)}) collective-permute-start(bf16[16,4480]{1,0:T(8,128)(2,1)} %get-tuple-element.54), channel_id=1, source_target_pairs={{0,46},{1,239},{2,44},{3,237},{4,50},{5,243},{6,48},{7,241},{8,54}... | collective-permute-start | bytes 430088 | tf_op jit(solution)/shard_map/ppermute | solution.py:283
  124.5 0.3 collective-permute-done.11.refs_8_
  124.8 6.7 %collective-permute-start.16 = (bf16[16,4480]{1,0:T(8,128)(2,1)}, bf16[16,4480]{1,0:T(8,128)(2,1)S(1)}, u32[]{:S(2)}, u32[]{:S(2)}) collective-permute-start(bf16[16,4480]{1,0:T(8,128)(2,1)} %get-tuple-element.55), channel_id=1, source_target_pairs={{0,58},{1,251},{2,56},{3,249},{4,62},{5,255},{6,60},{7,253},{8,34}... | collective-permute-start | bytes 430088 | tf_op jit(solution)/shard_map/ppermute | solution.py:283
  131.5 0.0 collective-permute-done.12.refs_9_
  131.5 3.4 %collective-permute-start.17 = (bf16[16,4480]{1,0:T(8,128)(2,1)}, bf16[16,4480]{1,0:T(8,128)(2,1)S(1)}, u32[]{:S(2)}, u32[]{:S(2)}) collective-permute-start(bf16[16,4480]{1,0:T(8,128)(2,1)} %get-tuple-element.56), channel_id=1, source_target_pairs={{0,40},{1,233},{2,42},{3,235},{4,44},{5,237},{6,46},{7,239},{8,48}... | collective-permute-start | bytes 430088 | tf_op jit(solution)/shard_map/ppermute | solution.py:283
  134.8 0.0 collective-permute-done.13.refs_10_
  134.8 0.4 collective-permute-start.18
  135.2 0.0 collective-permute-done.14.refs_11_
  135.2 0.0 collective-permute-done.15.refs_12_
  135.2 9.4 %collective-permute-done.16.refs_13_ = bf16[16,4480]{1,0:T(8,128)(2,1)S(1)} collective-permute-done((bf16[16,4480]{1,0:T(8,128)(2,1)}, bf16[16,4480]{1,0:T(8,128)(2,1)S(1)}, u32[]{:S(2)}, u32[]{:S(2)}) %collective-permute-start.16) | collective-permute-done | bytes 143392 | tf_op jit(solution)/shard_map/ppermute | solution.py:283
  144.6 0.0 collective-permute-done.17.refs_14_
  144.6 0.0 collective-permute-done.18.refs_15_
  144.6 1.6 %shard_map.88 = bf16[64,3584]{1,0:T(8,128)(2,1)S(1)} custom-call(s32[1]{0:T(128)} %bitcast.core, bf16[144,3584]{1,0:T(8,128)(2,1)S(1)} %collective-permute-done.carried, bf16[16,4480]{1,0:T(8,128)(2,1)S(1)} %collective-permute-done.3.refs_0_, bf16[16,4480]{1,0:T(8,128)(2,1)S(1)} %collective-permute-done.4.refs_1_, ...), custom_call_target="tpu_custom_call" | custom-call | tf_op jit(solution)/shard_map/pallas_call | solution.py:255
  146.2 0.1 collective-permute-start.19
  146.3 2.4 %shard_map.89 = (bf16[64,3584]{1,0:T(8,128)(2,1)}, bf16[64,3584]{1,0:T(8,128)(2,1)}) custom-call(s32[1]{0:T(128)} %bitcast.core, bf16[144,3584]{1,0:T(8,128)(2,1)S(1)} %collective-permute-done.carried, bf16[16,4480]{1,0:T(8,128)(2,1)S(1)} %collective-permute-done.3.refs_0_, bf16[16,4480]{1,0:T(8,128)(2,1)S(1)} %collective-permute-done.4.refs_1_, ...), custom_call_target="tpu_custom_call" | custom-call | tf_op jit(solution)/shard_map/pallas_call | solution.py:262
  148.7 6.1 %collective-permute-done.19.came = bf16[64,3584]{1,0:T(8,128)(2,1)S(1)} collective-permute-done((bf16[64,3584]{1,0:T(8,128)(2,1)S(1)}, bf16[64,3584]{1,0:T(8,128)(2,1)S(1)}, u32[]{:S(2)}, u32[]{:S(2)}) %collective-permute-start.19) | collective-permute-done | bytes 458784 | tf_op jit(solution)/shard_map/ppermute | solution.py:283
  154.8 0.8 shard_map.90
Async XLA Ops:
  4.8 67.7 %collective-permute-start.1 = (bf16[3584,1024]{1,0:T(8,128)(2,1)}, bf16[3584,1024]{1,0:T(8,128)(2,1)}, u32[]{:S(2)}, u32[]{:S(2)}) collective-permute-start(bf16[3584,1024]{1,0:T(8,128)(2,1)} %bitcast.18), channel_id=1, source_target_pairs={{0,1},{1,0},{2,3},{3,2},{4,5},{5,4},{6,7},{7,6},{8,9},{9,8},{10,11... | collective-permute-start | bytes 22020104 | tf_op jit(solution)/shard_map/ppermute | solution.py:283
  8.2 64.4 %all-to-all-start = ((bf16[16,16,4480]{2,1,0:T(8,128)(2,1)}), bf16[16,16,4480]{2,1,0:T(8,128)(2,1)S(1)}, u32[]{:S(2)}, u32[]{:S(2)}) async-start(bf16[16,16,4480]{2,1,0:T(8,128)(2,1)} %bitcast.22), calls=%async_computation | async-start | bytes 4587520 | tf_op jit(solution)/shard_map/all_to_all | solution.py:295
  17.2 30.1 %collective-permute-start.2 = (bf16[512,3584]{1,0:T(8,128)(2,1)}, bf16[512,3584]{1,0:T(8,128)(2,1)}, u32[]{:S(2)}, u32[]{:S(2)}) collective-permute-start(bf16[512,3584]{1,0:T(8,128)(2,1)} %bitcast.20), channel_id=1, source_target_pairs={{0,1},{1,0},{2,3},{3,2},{4,5},{5,4},{6,7},{7,6},{8,9},{9,8},{10,11... | collective-permute-start | bytes 11010056 | tf_op jit(solution)/shard_map/ppermute | solution.py:283
  17.6 29.7 %collective-permute-start = (bf16[144,3584]{1,0:T(8,128)(2,1)}, bf16[144,3584]{1,0:T(8,128)(2,1)S(1)}, u32[]{:S(2)}, u32[]{:S(2)}) collective-permute-start(bf16[144,3584]{1,0:T(8,128)(2,1)} %get-tuple-element.33), channel_id=1, source_target_pairs={{0,32},{1,225},{2,34},{3,227},{4,36},{5,229},{6,38},{7,231},{8,40}... | collective-permute-start | bytes 3096584 | tf_op jit(solution)/shard_map/ppermute | solution.py:283
  84.9 12.3 %collective-permute-start.3 = (bf16[16,4480]{1,0:T(8,128)(2,1)S(1)}, bf16[16,4480]{1,0:T(8,128)(2,1)S(1)}, u32[]{:S(2)}, u32[]{:S(2)}) collective-permute-start(bf16[16,4480]{1,0:T(8,128)(2,1)S(1)} %get-tuple-element.42), channel_id=1, source_target_pairs={{0,60},{1,253},{2,62},{3,255},{4,32},{5,225},{6,34},{7,227},{8,36}... | collective-permute-start | bytes 430088 | tf_op jit(solution)/shard_map/ppermute | solution.py:283
  87.2 16.1 %collective-permute-start.4 = (bf16[16,4480]{1,0:T(8,128)(2,1)S(1)}, bf16[16,4480]{1,0:T(8,128)(2,1)S(1)}, u32[]{:S(2)}, u32[]{:S(2)}) collective-permute-start(bf16[16,4480]{1,0:T(8,128)(2,1)S(1)} %get-tuple-element.43), channel_id=1, source_target_pairs={{0,50},{1,243},{2,48},{3,241},{4,54},{5,247},{6,52},{7,245},{8,58}... | collective-permute-start | bytes 430088 | tf_op jit(solution)/shard_map/ppermute | solution.py:283
  92.9 13.2 %collective-permute-start.5 = (bf16[16,4480]{1,0:T(8,128)(2,1)S(1)}, bf16[16,4480]{1,0:T(8,128)(2,1)S(1)}, u32[]{:S(2)}, u32[]{:S(2)}) collective-permute-start(bf16[16,4480]{1,0:T(8,128)(2,1)S(1)} %get-tuple-element.44), channel_id=1, source_target_pairs={{0,36},{1,229},{2,38},{3,231},{4,40},{5,233},{6,42},{7,235},{8,44}... | collective-permute-start | bytes 430088 | tf_op jit(solution)/shard_map/ppermute | solution.py:283
  93.0 16.6 %collective-permute-start.6 = (bf16[16,4480]{1,0:T(8,128)(2,1)S(1)}, bf16[16,4480]{1,0:T(8,128)(2,1)S(1)}, u32[]{:S(2)}, u32[]{:S(2)}) collective-permute-start(bf16[16,4480]{1,0:T(8,128)(2,1)S(1)} %get-tuple-element.45), channel_id=1, source_target_pairs={{0,52},{1,245},{2,54},{3,247},{4,56},{5,249},{6,58},{7,251},{8,60}... | collective-permute-start | bytes 430088 | tf_op jit(solution)/shard_map/ppermute | solution.py:283
  94.6 17.6 %collective-permute-start.7 = (bf16[16,4480]{1,0:T(8,128)(2,1)S(1)}, bf16[16,4480]{1,0:T(8,128)(2,1)S(1)}, u32[]{:S(2)}, u32[]{:S(2)}) collective-permute-start(bf16[16,4480]{1,0:T(8,128)(2,1)S(1)} %get-tuple-element.46), channel_id=1, source_target_pairs={{0,34},{1,227},{2,32},{3,225},{4,38},{5,231},{6,36},{7,229},{8,42}... | collective-permute-start | bytes 430088 | tf_op jit(solution)/shard_map/ppermute | solution.py:283
  97.2 21.1 %collective-permute-start.8 = (bf16[16,4480]{1,0:T(8,128)(2,1)S(1)}, bf16[16,4480]{1,0:T(8,128)(2,1)S(1)}, u32[]{:S(2)}, u32[]{:S(2)}) collective-permute-start(bf16[16,4480]{1,0:T(8,128)(2,1)S(1)} %get-tuple-element.47), channel_id=1, source_target_pairs={{0,44},{1,237},{2,46},{3,239},{4,48},{5,241},{6,50},{7,243},{8,52}... | collective-permute-start | bytes 430088 | tf_op jit(solution)/shard_map/ppermute | solution.py:283
  103.3 15.0 %collective-permute-start.9 = (bf16[16,4480]{1,0:T(8,128)(2,1)S(1)}, bf16[16,4480]{1,0:T(8,128)(2,1)S(1)}, u32[]{:S(2)}, u32[]{:S(2)}) collective-permute-start(bf16[16,4480]{1,0:T(8,128)(2,1)S(1)} %get-tuple-element.48), channel_id=1, source_target_pairs={{0,56},{1,249},{2,58},{3,251},{4,60},{5,253},{6,62},{7,255},{8,32}... | collective-permute-start | bytes 430088 | tf_op jit(solution)/shard_map/ppermute | solution.py:283
  106.1 15.7 %collective-permute-start.10 = (bf16[16,4480]{1,0:T(8,128)(2,1)S(1)}, bf16[16,4480]{1,0:T(8,128)(2,1)S(1)}, u32[]{:S(2)}, u32[]{:S(2)}) collective-permute-start(bf16[16,4480]{1,0:T(8,128)(2,1)S(1)} %get-tuple-element.49), channel_id=1, source_target_pairs={{0,42},{1,235},{2,40},{3,233},{4,46},{5,239},{6,44},{7,237},{8,50}... | collective-permute-start | bytes 430088 | tf_op jit(solution)/shard_map/ppermute | solution.py:283
  109.6 15.2 %collective-permute-start.11 = (bf16[16,4480]{1,0:T(8,128)(2,1)S(1)}, bf16[16,4480]{1,0:T(8,128)(2,1)S(1)}, u32[]{:S(2)}, u32[]{:S(2)}) collective-permute-start(bf16[16,4480]{1,0:T(8,128)(2,1)S(1)} %get-tuple-element.50), channel_id=1, source_target_pairs={{0,48},{1,241},{2,50},{3,243},{4,52},{5,245},{6,54},{7,247},{8,56}... | collective-permute-start | bytes 430088 | tf_op jit(solution)/shard_map/ppermute | solution.py:283
  112.2 19.3 %collective-permute-start.12 = (bf16[16,4480]{1,0:T(8,128)(2,1)S(1)}, bf16[16,4480]{1,0:T(8,128)(2,1)S(1)}, u32[]{:S(2)}, u32[]{:S(2)}) collective-permute-start(bf16[16,4480]{1,0:T(8,128)(2,1)S(1)} %get-tuple-element.51), channel_id=1, source_target_pairs={{0,62},{1,255},{2,60},{3,253},{4,34},{5,227},{6,32},{7,225},{8,38}... | collective-permute-start | bytes 430088 | tf_op jit(solution)/shard_map/ppermute | solution.py:283
  118.3 16.6 %collective-permute-start.13 = (bf16[16,4480]{1,0:T(8,128)(2,1)S(1)}, bf16[16,4480]{1,0:T(8,128)(2,1)S(1)}, u32[]{:S(2)}, u32[]{:S(2)}) collective-permute-start(bf16[16,4480]{1,0:T(8,128)(2,1)S(1)} %get-tuple-element.52), channel_id=1, source_target_pairs={{0,38},{1,231},{2,36},{3,229},{4,42},{5,235},{6,40},{7,233},{8,46}... | collective-permute-start | bytes 430088 | tf_op jit(solution)/shard_map/ppermute | solution.py:283
  118.3 16.9 %collective-permute-start.14 = (bf16[16,4480]{1,0:T(8,128)(2,1)}, bf16[16,4480]{1,0:T(8,128)(2,1)S(1)}, u32[]{:S(2)}, u32[]{:S(2)}) collective-permute-start(bf16[16,4480]{1,0:T(8,128)(2,1)} %get-tuple-element.53), channel_id=1, source_target_pairs={{0,54},{1,247},{2,52},{3,245},{4,58},{5,251},{6,56},{7,249},{8,62}... | collective-permute-start | bytes 430088 | tf_op jit(solution)/shard_map/ppermute | solution.py:283
  121.7 13.5 %collective-permute-start.15 = (bf16[16,4480]{1,0:T(8,128)(2,1)}, bf16[16,4480]{1,0:T(8,128)(2,1)S(1)}, u32[]{:S(2)}, u32[]{:S(2)}) collective-permute-start(bf16[16,4480]{1,0:T(8,128)(2,1)} %get-tuple-element.54), channel_id=1, source_target_pairs={{0,46},{1,239},{2,44},{3,237},{4,50},{5,243},{6,48},{7,241},{8,54}... | collective-permute-start | bytes 430088 | tf_op jit(solution)/shard_map/ppermute | solution.py:283
  124.8 19.8 %collective-permute-start.16 = (bf16[16,4480]{1,0:T(8,128)(2,1)}, bf16[16,4480]{1,0:T(8,128)(2,1)S(1)}, u32[]{:S(2)}, u32[]{:S(2)}) collective-permute-start(bf16[16,4480]{1,0:T(8,128)(2,1)} %get-tuple-element.55), channel_id=1, source_target_pairs={{0,58},{1,251},{2,56},{3,249},{4,62},{5,255},{6,60},{7,253},{8,34}... | collective-permute-start | bytes 430088 | tf_op jit(solution)/shard_map/ppermute | solution.py:283
  131.5 13.1 %collective-permute-start.17 = (bf16[16,4480]{1,0:T(8,128)(2,1)}, bf16[16,4480]{1,0:T(8,128)(2,1)S(1)}, u32[]{:S(2)}, u32[]{:S(2)}) collective-permute-start(bf16[16,4480]{1,0:T(8,128)(2,1)} %get-tuple-element.56), channel_id=1, source_target_pairs={{0,40},{1,233},{2,42},{3,235},{4,44},{5,237},{6,46},{7,239},{8,48}... | collective-permute-start | bytes 430088 | tf_op jit(solution)/shard_map/ppermute | solution.py:283
  134.8 9.7 %collective-permute-start.18 = (bf16[16,4480]{1,0:T(8,128)(2,1)S(1)}, bf16[16,4480]{1,0:T(8,128)(2,1)S(1)}, u32[]{:S(2)}, u32[]{:S(2)}) collective-permute-start(bf16[16,4480]{1,0:T(8,128)(2,1)S(1)} %get-tuple-element.57), channel_id=1, source_target_pairs={{0,32},{1,225},{2,34},{3,227},{4,36},{5,229},{6,38},{7,231},{8,40}... | collective-permute-start | bytes 430088 | tf_op jit(solution)/shard_map/ppermute | solution.py:283
  146.2 8.6 %collective-permute-start.19 = (bf16[64,3584]{1,0:T(8,128)(2,1)S(1)}, bf16[64,3584]{1,0:T(8,128)(2,1)S(1)}, u32[]{:S(2)}, u32[]{:S(2)}) collective-permute-start(bf16[64,3584]{1,0:T(8,128)(2,1)S(1)} %shard_map.88), channel_id=1, source_target_pairs={{0,192},{1,65},{2,194},{3,67},{4,196},{5,69},{6,198},{7,71},{8,200... | collective-permute-start | bytes 1376264 | tf_op jit(solution)/shard_map/ppermute | solution.py:283

commit v3 on v2

--- a/solution.py
+++ b/solution.py
@@ -196,14 +196,14 @@
     )(place, recv, *(pltpu.with_memory_space_constraint(w, pltpu.HBM) for w in (*ups, *downs)))
 
 
-def summed(at, carried, blocks, main_all, rest_all, out):
+def summed(at, carried, blocks, main_all, rest_all, out, quarters):
     take = (iota((TOK, HALF), 0) == iota((TOK, HALF), 1) + at).astype(BF16)
     meta = jnp.dot(carried[TOK : TOK + META, 0:TOK], take, preferred_element_type=F32)
     numbers = [meta[k : k + 1, :].astype(jnp.int32) for k in range(2)]
     ranks = [meta[2 + k : 3 + k, :].astype(jnp.int32) for k in range(2)]
     main, rest = slot_masks(numbers, ranks, HALF)
     for i in range(CHIPS):
-        main_all[i * MAIN : (i + 1) * MAIN, :] = blocks[i][:, 0:D]
+        main_all[i * MAIN : (i + 1) * MAIN, :] = blocks[i][:, quarters[0] * QUART : (quarters[-1] + 1) * QUART]
         rest_all[i * MAIN : (i + 1) * MAIN, :] = blocks[i][:, D:WIDE]
 
     def weighed(masks):
@@ -218,60 +218,65 @@
         return sum(lax.dot_general(m, rows, dims, preferred_element_type=F32) for m in mats)
 
     main_w = weighed(main)
-    for j in range(4):
-        cols = slice(j * QUART, (j + 1) * QUART)
-        mixed = product(main_w, main_all[:, cols]) + product(weighed(rest[j]), rest_all[...])
-        out[:, cols] = (carried[pl.ds(at, HALF), cols].astype(F32) + mixed).astype(BF16)
-
-
-def going_kernel(core, carried, *refs):
+    for n, j in enumerate(quarters):
+        near, cols = slice(n * QUART, (n + 1) * QUART), slice(j * QUART, (j + 1) * QUART)
+        mixed = product(main_w, main_all[:, near]) + product(weighed(rest[j]), rest_all[...])
+        out[:, near] = (carried[pl.ds(at, HALF), cols].astype(F32) + mixed).astype(BF16)
+
+
+def going_kernel(quarters, core, carried, *refs):
     at = pl.multiple_of(HALF * (1 - core[0]), HALF)
-    summed(at, carried, refs[:CHIPS], refs[CHIPS + 1], refs[CHIPS + 2], refs[CHIPS])
-
-
-def stored(core, rows, targets, sem):
+    summed(at, carried, refs[:CHIPS], refs[CHIPS + 1], refs[CHIPS + 2], refs[CHIPS], quarters)
+
+
+def stored(core, pairs, sems):
     for c in range(2):
 
         @pl.when(core[0] == c)
         def _():
-            copy = pltpu.make_async_copy(rows, targets[c], sem)
-            copy.start()
-            copy.wait()
+            copies = [pltpu.make_async_copy(rows, targets[c], sems.at[n]) for n, (rows, targets) in enumerate(pairs)]
+            for copy in copies:
+                copy.start()
+            for copy in copies:
+                copy.wait()
 
 
 def staying_kernel(core, carried, *refs):
     blocks, (fwd, bwd, main_all, rest_all, rows, sem) = refs[:CHIPS], refs[CHIPS:]
-    summed(pl.multiple_of(HALF * core[0], HALF), carried, blocks, main_all, rest_all, rows)
-    stored(core, rows, (fwd, bwd), sem)
-
-
-def came_kernel(core, came, fwd_held, bwd_held, fwd, bwd, sem):
-    stored(core, came, (bwd, fwd), sem)
-
-
-def going(core, carried, blocks):
-    scratch = [pltpu.VMEM((CHIPS * MAIN, D), BF16), pltpu.VMEM((CHIPS * MAIN, QUART), BF16)]
-    out = jax.ShapeDtypeStruct((HALF, D), BF16)
-    return call(going_kernel, out, [SMEM] + [VMEM] * (CHIPS + 1), VMEM, scratch)(core, carried, *blocks)
+    summed(pl.multiple_of(HALF * core[0], HALF), carried, blocks, main_all, rest_all, rows, range(4))
+    stored(core, [(rows, (fwd, bwd))], sem)
+
+
+def came_kernel(core, low, high, fwd_held, bwd_held, fwd, bwd, sems):
+    cut = D // 2
+    pairs = [(low, (bwd.at[:, 0:cut], fwd.at[:, 0:cut])), (high, (bwd.at[:, cut:D], fwd.at[:, cut:D]))]
+    stored(core, pairs, sems)
+
+
+def going(core, carried, blocks, quarters):
+    width = len(quarters) * QUART
+    scratch = [pltpu.VMEM((CHIPS * MAIN, width), BF16), pltpu.VMEM((CHIPS * MAIN, QUART), BF16)]
+    kernel = functools.partial(going_kernel, quarters)
+    return call(kernel, jax.ShapeDtypeStruct((HALF, width), BF16), [SMEM] + [VMEM] * (CHIPS + 1), VMEM, scratch)(core, carried, *blocks)
 
 
 def staying(core, carried, blocks):
     scratch = [pltpu.VMEM((CHIPS * MAIN, D), BF16), pltpu.VMEM((CHIPS * MAIN, QUART), BF16)]
-    scratch += [pltpu.VMEM((HALF, D), BF16), pltpu.SemaphoreType.DMA]
+    scratch += [pltpu.VMEM((HALF, D), BF16), pltpu.SemaphoreType.DMA((1,))]
     out = [pltpu.HBM((HALF, D), BF16)] * 2
     return call(staying_kernel, out, [SMEM] + [VMEM] * (CHIPS + 1), [HBM] * 2, scratch)(core, carried, *blocks)
 
 
-def arrive(core, came, fwd, bwd):
+def arrive(core, low, high, fwd, bwd):
     return pl.pallas_call(
         came_kernel,
         out_shape=[pltpu.HBM((HALF, D), BF16)] * 2,
-        in_specs=[SMEM, VMEM, HBM, HBM],
+        in_specs=[SMEM, VMEM, VMEM, HBM, HBM],
         out_specs=[HBM] * 2,
-        scratch_shapes=[pltpu.SemaphoreType.DMA],
-        input_output_aliases={2: 0, 3: 1},
+        scratch_shapes=[pltpu.SemaphoreType.DMA((2,))],
+        input_output_aliases={3: 0, 4: 1},
         compiler_params=pltpu.CompilerParams(vmem_limit_bytes=4 * 2**20),
-    )(core, came, fwd, bwd)
+    )(core, low, high, fwd, bwd)
 
 
 def moved(block, route):
@@ -300,8 +305,10 @@
     for (dz, dx), block in zip(ORDER, expert(place, recv, ups, downs)):
         back.append(moved(block, lambda p, z, xh, c, dz=dz, dx=dx: (p + 1 - 2 * c, z - dz, xh + dx, c)))
     core = (spot % 2).astype(jnp.int32).reshape(1)
-    came = moved(going(core, beside, back), lambda p, z, xh, c: (p - 2 + 4 * c, z, xh, c))
-    fwd_next, bwd_next = arrive(core, came, *staying(core, beside, back))
+    came = [
+        moved(going(core, beside, back, quarters), lambda p, z, xh, c: (p - 2 + 4 * c, z, xh, c)) for quarters in (range(0, 2), range(2, 4))
+    ]
+    fwd_next, bwd_next = arrive(core, *came, *staying(core, beside, back))
     return fwd_next[None], bwd_next[None]
 
 

time: 157 us -> 157 us (level)
  waiting for transfers between devices: 68 us -> 63.3 us
  starting transfers between devices: 65.6 us -> 69 us
    ppermute x20 -> x21, waiting for transfers between devices: 42.7 us -> 38 us  [moved(): return lax.ppermute(block, ('pipe', 'expert'), pairs)]
    ppermute x20 -> x21, starting transfers between devices: 56.6 us -> 59.9 us  [moved(): return lax.ppermute(block, ('pipe', 'expert'), pairs)]
  transfers between devices with their start and end apart: 21 -> 22, of which waited for: 5 -> 7; matrix products, arithmetic and copies ran while one was open for 0% -> 0% of each run, Pallas kernels for 2% -> 2%
where the time goes in v3:
time: 157 us; the launch traced here: 155 us
  starting transfers between devices  69 us (44%)
  waiting for transfers between devices  63.3 us (40%)
  Pallas kernels  21.6 us (14%)
    ppermute x21, starting transfers between devices, moved(): return lax.ppermute(block, ('pipe', 'expert'), pairs)  59.9 us
    ppermute x21, waiting for transfers between devices, moved(): return lax.ppermute(block, ('pipe', 'expert'), pairs)  38 us
    all_to_all x1, waiting for transfers between devices, on_device(): lax.all_to_all(send, 'expert', split_axis=0, concat_axis=0, tiled=True, a...  25.3 us
    pallas_call x1, Pallas kernels, expert(): call(expert_kernel, [shape((MAIN, WIDE), BF16)] * CHIPS, [SMEM, VMEM] + [...  12.3 us
    all_to_all x1, starting transfers between devices, on_device(): lax.all_to_all(send, 'expert', split_axis=0, concat_axis=0, tiled=True, a...  9.01 us
    pallas_call x1, Pallas kernels, build(): call(build_kernel, [pltpu.HBM((CHIPS * MAIN, WIDE), BF16), pltpu.HBM((TOK...  4.13 us
  transfers between devices with their start and end apart: 22, of which 7 were waited for; matrix products, arithmetic and copies ran while one was open for 0% of the time, Pallas kernels for 2%

profile of v3, /device:TPU:1, one launch (start us, length us, event | category | flops | bytes accessed | tf_op | source)
XLA Modules:
  0.0 154.8 jit_solution(16292705159019896478)
XLA Ops:
  0.7 0.1 pad_add_fusion.place
  0.7 4.1 %shard_map.86 = (bf16[256,4480]{1,0:T(8,128)(2,1)}, bf16[144,3584]{1,0:T(8,128)(2,1)}) custom-call(s32[2]{0:T(128)S(1)} %pad_add_fusion.place, bf16[64,3584]{1,0:T(8,128)(2,1)} %bitcast.23, bf16[64,3584]{1,0:T(8,128)(2,1)} %bitcast.24, s32[2,128]{1,0:T(2,128)} %bitcast.27, f32[2,128]{1,0:T(2,128)} %bitcast.28, f32[1,3584]{1,0:T(1,128)} %gain_hbm.1), custom_call_target="tpu_custom_call" | custom-call | tf_op jit(solution)/shard_map/pallas_call | solution.py:112
  4.9 3.3 %collective-permute-start.1 = (bf16[3584,1024]{1,0:T(8,128)(2,1)}, bf16[3584,1024]{1,0:T(8,128)(2,1)}, u32[]{:S(2)}, u32[]{:S(2)}) collective-permute-start(bf16[3584,1024]{1,0:T(8,128)(2,1)} %bitcast.18), channel_id=1, source_target_pairs={{0,1},{1,0},{2,3},{3,2},{4,5},{5,4},{6,7},{7,6},{8,9},{9,8},{10,11... | collective-permute-start | bytes 22020104 | tf_op jit(solution)/shard_map/ppermute | solution.py:288
  8.2 9.0 %all-to-all-start = ((bf16[16,16,4480]{2,1,0:T(8,128)(2,1)}), bf16[16,16,4480]{2,1,0:T(8,128)(2,1)S(1)}, u32[]{:S(2)}, u32[]{:S(2)}) async-start(bf16[16,16,4480]{2,1,0:T(8,128)(2,1)} %bitcast.22), calls=%async_computation | async-start | bytes 4587520 | tf_op jit(solution)/shard_map/all_to_all | solution.py:300
  17.2 0.4 collective-permute-start.2
  17.6 2.8 %collective-permute-start = (bf16[144,3584]{1,0:T(8,128)(2,1)}, bf16[144,3584]{1,0:T(8,128)(2,1)S(1)}, u32[]{:S(2)}, u32[]{:S(2)}) collective-permute-start(bf16[144,3584]{1,0:T(8,128)(2,1)} %get-tuple-element.33), channel_id=1, source_target_pairs={{0,32},{1,225},{2,34},{3,227},{4,36},{5,229},{6,38},{7,231},{8,40}... | collective-permute-start | bytes 3096584 | tf_op jit(solution)/shard_map/ppermute | solution.py:288
  20.4 26.9 %collective-permute-done.carried = bf16[144,3584]{1,0:T(8,128)(2,1)S(1)} collective-permute-done((bf16[144,3584]{1,0:T(8,128)(2,1)}, bf16[144,3584]{1,0:T(8,128)(2,1)S(1)}, u32[]{:S(2)}, u32[]{:S(2)}) %collective-permute-start) | collective-permute-done | bytes 1032224 | tf_op jit(solution)/shard_map/ppermute | solution.py:288
  47.3 0.0 collective-permute-done.2.refs_3_
  47.3 25.3 %all-to-all-done = bf16[16,16,4480]{2,1,0:T(8,128)(2,1)S(1)} async-done(((bf16[16,16,4480]{2,1,0:T(8,128)(2,1)}), bf16[16,16,4480]{2,1,0:T(8,128)(2,1)S(1)}, u32[]{:S(2)}, u32[]{:S(2)}) %all-to-all-start) | async-done | bytes 2293792 | tf_op jit(solution)/shard_map/all_to_all | solution.py:300
  72.6 0.0 collective-permute-done.1.refs_1_
  72.6 12.3 %shard_map.87 = (bf16[16,4480]{1,0:T(8,128)(2,1)S(1)}, bf16[16,4480]{1,0:T(8,128)(2,1)S(1)}, bf16[16,4480]{1,0:T(8,128)(2,1)S(1)}, bf16[16,4480]{1,0:T(8,128)(2,...) custom-call(s32[2]{0:T(128)S(1)} %pad_add_fusion.place, ...), custom_call_target="tpu_custom_call" | custom-call | tf_op jit(solution)/shard_map/pallas_call | solution.py:182
  84.9 2.3 %collective-permute-start.3 = (bf16[16,4480]{1,0:T(8,128)(2,1)S(1)}, bf16[16,4480]{1,0:T(8,128)(2,1)S(1)}, u32[]{:S(2)}, u32[]{:S(2)}) collective-permute-start(bf16[16,4480]{1,0:T(8,128)(2,1)S(1)} %get-tuple-element.42), channel_id=1, source_target_pairs={{0,60},{1,253},{2,62},{3,255},{4,32},{5,225},{6,34},{7,227},{8,36}... | collective-permute-start | bytes 430088 | tf_op jit(solution)/shard_map/ppermute | solution.py:288
  87.3 5.7 %collective-permute-start.4 = (bf16[16,4480]{1,0:T(8,128)(2,1)S(1)}, bf16[16,4480]{1,0:T(8,128)(2,1)S(1)}, u32[]{:S(2)}, u32[]{:S(2)}) collective-permute-start(bf16[16,4480]{1,0:T(8,128)(2,1)S(1)} %get-tuple-element.43), channel_id=1, source_target_pairs={{0,50},{1,243},{2,48},{3,241},{4,54},{5,247},{6,52},{7,245},{8,58}... | collective-permute-start | bytes 430088 | tf_op jit(solution)/shard_map/ppermute | solution.py:288
  93.0 0.1 collective-permute-start.5
  93.0 1.6 %collective-permute-start.6 = (bf16[16,4480]{1,0:T(8,128)(2,1)S(1)}, bf16[16,4480]{1,0:T(8,128)(2,1)S(1)}, u32[]{:S(2)}, u32[]{:S(2)}) collective-permute-start(bf16[16,4480]{1,0:T(8,128)(2,1)S(1)} %get-tuple-element.45), channel_id=1, source_target_pairs={{0,52},{1,245},{2,54},{3,247},{4,56},{5,249},{6,58},{7,251},{8,60}... | collective-permute-start | bytes 430088 | tf_op jit(solution)/shard_map/ppermute | solution.py:288
  94.7 2.6 %collective-permute-start.7 = (bf16[16,4480]{1,0:T(8,128)(2,1)S(1)}, bf16[16,4480]{1,0:T(8,128)(2,1)S(1)}, u32[]{:S(2)}, u32[]{:S(2)}) collective-permute-start(bf16[16,4480]{1,0:T(8,128)(2,1)S(1)} %get-tuple-element.46), channel_id=1, source_target_pairs={{0,34},{1,227},{2,32},{3,225},{4,38},{5,231},{6,36},{7,229},{8,42}... | collective-permute-start | bytes 430088 | tf_op jit(solution)/shard_map/ppermute | solution.py:288
  97.2 0.0 collective-permute-done.3.refs_0_
  97.3 6.1 %collective-permute-start.8 = (bf16[16,4480]{1,0:T(8,128)(2,1)S(1)}, bf16[16,4480]{1,0:T(8,128)(2,1)S(1)}, u32[]{:S(2)}, u32[]{:S(2)}) collective-permute-start(bf16[16,4480]{1,0:T(8,128)(2,1)S(1)} %get-tuple-element.47), channel_id=1, source_target_pairs={{0,44},{1,237},{2,46},{3,239},{4,48},{5,241},{6,50},{7,243},{8,52}... | collective-permute-start | bytes 430088 | tf_op jit(solution)/shard_map/ppermute | solution.py:288
  103.4 0.0 collective-permute-done.4.refs_1_
  103.4 2.7 %collective-permute-start.9 = (bf16[16,4480]{1,0:T(8,128)(2,1)S(1)}, bf16[16,4480]{1,0:T(8,128)(2,1)S(1)}, u32[]{:S(2)}, u32[]{:S(2)}) collective-permute-start(bf16[16,4480]{1,0:T(8,128)(2,1)S(1)} %get-tuple-element.48), channel_id=1, source_target_pairs={{0,56},{1,249},{2,58},{3,251},{4,60},{5,253},{6,62},{7,255},{8,32}... | collective-permute-start | bytes 430088 | tf_op jit(solution)/shard_map/ppermute | solution.py:288
  106.1 0.0 collective-permute-done.5.refs_2_
  106.1 3.5 %collective-permute-start.10 = (bf16[16,4480]{1,0:T(8,128)(2,1)S(1)}, bf16[16,4480]{1,0:T(8,128)(2,1)S(1)}, u32[]{:S(2)}, u32[]{:S(2)}) collective-permute-start(bf16[16,4480]{1,0:T(8,128)(2,1)S(1)} %get-tuple-element.49), channel_id=1, source_target_pairs={{0,42},{1,235},{2,40},{3,233},{4,46},{5,239},{6,44},{7,237},{8,50}... | collective-permute-start | bytes 430088 | tf_op jit(solution)/shard_map/ppermute | solution.py:288
  109.6 0.0 collective-permute-done.6.refs_3_
  109.6 2.6 %collective-permute-start.11 = (bf16[16,4480]{1,0:T(8,128)(2,1)S(1)}, bf16[16,4480]{1,0:T(8,128)(2,1)S(1)}, u32[]{:S(2)}, u32[]{:S(2)}) collective-permute-start(bf16[16,4480]{1,0:T(8,128)(2,1)S(1)} %get-tuple-element.50), channel_id=1, source_target_pairs={{0,48},{1,241},{2,50},{3,243},{4,52},{5,245},{6,54},{7,247},{8,56}... | collective-permute-start | bytes 430088 | tf_op jit(solution)/shard_map/ppermute | solution.py:288
  112.2 0.0 collective-permute-done.7.refs_4_
  112.2 6.1 %collective-permute-start.12 = (bf16[16,4480]{1,0:T(8,128)(2,1)S(1)}, bf16[16,4480]{1,0:T(8,128)(2,1)S(1)}, u32[]{:S(2)}, u32[]{:S(2)}) collective-permute-start(bf16[16,4480]{1,0:T(8,128)(2,1)S(1)} %get-tuple-element.51), channel_id=1, source_target_pairs={{0,62},{1,255},{2,60},{3,253},{4,34},{5,227},{6,32},{7,225},{8,38}... | collective-permute-start | bytes 430088 | tf_op jit(solution)/shard_map/ppermute | solution.py:288
  118.4 0.0 collective-permute-done.8.refs_5_
  118.4 0.0 collective-permute-done.9.refs_6_
  118.4 4.2 %collective-permute-start.14 = (bf16[16,4480]{1,0:T(8,128)(2,1)}, bf16[16,4480]{1,0:T(8,128)(2,1)S(1)}, u32[]{:S(2)}, u32[]{:S(2)}) collective-permute-start(bf16[16,4480]{1,0:T(8,128)(2,1)} %get-tuple-element.53), channel_id=1, source_target_pairs={{0,54},{1,247},{2,52},{3,245},{4,58},{5,251},{6,56},{7,249},{8,62}... | collective-permute-start | bytes 430088 | tf_op jit(solution)/shard_map/ppermute | solution.py:288
  122.6 0.0 collective-permute-done.10.refs_7_
  122.6 1.9 %collective-permute-start.15 = (bf16[16,4480]{1,0:T(8,128)(2,1)}, bf16[16,4480]{1,0:T(8,128)(2,1)S(1)}, u32[]{:S(2)}, u32[]{:S(2)}) collective-permute-start(bf16[16,4480]{1,0:T(8,128)(2,1)} %get-tuple-element.54), channel_id=1, source_target_pairs={{0,46},{1,239},{2,44},{3,237},{4,50},{5,243},{6,48},{7,241},{8,54}... | collective-permute-start | bytes 430088 | tf_op jit(solution)/shard_map/ppermute | solution.py:288
  124.5 0.3 collective-permute-done.11.refs_8_
  124.8 6.5 %collective-permute-start.16 = (bf16[16,4480]{1,0:T(8,128)(2,1)}, bf16[16,4480]{1,0:T(8,128)(2,1)S(1)}, u32[]{:S(2)}, u32[]{:S(2)}) collective-permute-start(bf16[16,4480]{1,0:T(8,128)(2,1)} %get-tuple-element.55), channel_id=1, source_target_pairs={{0,58},{1,251},{2,56},{3,249},{4,62},{5,255},{6,60},{7,253},{8,34}... | collective-permute-start | bytes 430088 | tf_op jit(solution)/shard_map/ppermute | solution.py:288
  131.3 6.7 %collective-permute-start.17 = (bf16[16,4480]{1,0:T(8,128)(2,1)}, bf16[16,4480]{1,0:T(8,128)(2,1)S(1)}, u32[]{:S(2)}, u32[]{:S(2)}) collective-permute-start(bf16[16,4480]{1,0:T(8,128)(2,1)} %get-tuple-element.56), channel_id=1, source_target_pairs={{0,40},{1,233},{2,42},{3,235},{4,44},{5,237},{6,46},{7,239},{8,48}... | collective-permute-start | bytes 430088 | tf_op jit(solution)/shard_map/ppermute | solution.py:288
  138.0 0.0 collective-permute-done.13.refs_10_
  138.0 0.0 collective-permute-start.18
  138.0 0.0 collective-permute-done.14.refs_11_
  138.1 6.1 %collective-permute-done.16.refs_13_ = bf16[16,4480]{1,0:T(8,128)(2,1)S(1)} collective-permute-done((bf16[16,4480]{1,0:T(8,128)(2,1)}, bf16[16,4480]{1,0:T(8,128)(2,1)S(1)}, u32[]{:S(2)}, u32[]{:S(2)}) %collective-permute-start.16) | collective-permute-done | bytes 143392 | tf_op jit(solution)/shard_map/ppermute | solution.py:288
  144.1 0.0 collective-permute-done.17.refs_14_
  144.1 0.2 collective-permute-done.18.refs_15_
  144.3 1.0 shard_map.88
  145.3 0.1 collective-permute-start.19
  145.4 1.0 shard_map.89
  146.4 0.6 collective-permute-start.20
  147.0 2.4 %shard_map.90 = (bf16[64,3584]{1,0:T(8,128)(2,1)}, bf16[64,3584]{1,0:T(8,128)(2,1)}) custom-call(s32[1]{0:T(128)} %bitcast.core, bf16[144,3584]{1,0:T(8,128)(2,1)S(1)} %collective-permute-done.carried, bf16[16,4480]{1,0:T(8,128)(2,1)S(1)} %collective-permute-done.3.refs_0_, bf16[16,4480]{1,0:T(8,128)(2,1)S(1)} %collective-permute-done.4.refs_1_, ...), custom_call_target="tpu_custom_call" | custom-call | tf_op jit(solution)/shard_map/pallas_call | solution.py:267
  149.4 2.0 %collective-permute-done.19.low = bf16[64,1792]{1,0:T(8,128)(2,1)S(1)} collective-permute-done((bf16[64,1792]{1,0:T(8,128)(2,1)S(1)}, bf16[64,1792]{1,0:T(8,128)(2,1)S(1)}, u32[]{:S(2)}, u32[]{:S(2)}) %collective-permute-start.19) | collective-permute-done | bytes 229408 | tf_op jit(solution)/shard_map/ppermute | solution.py:288
  151.4 2.5 %collective-permute-done.20.high = bf16[64,1792]{1,0:T(8,128)(2,1)S(1)} collective-permute-done((bf16[64,1792]{1,0:T(8,128)(2,1)S(1)}, bf16[64,1792]{1,0:T(8,128)(2,1)S(1)}, u32[]{:S(2)}, u32[]{:S(2)}) %collective-permute-start.20) | collective-permute-done | bytes 229408 | tf_op jit(solution)/shard_map/ppermute | solution.py:288
  153.9 0.8 shard_map.91
  (3 shorter events, 0.0 us)
Async XLA Ops:
  4.9 67.7 %collective-permute-start.1 = (bf16[3584,1024]{1,0:T(8,128)(2,1)}, bf16[3584,1024]{1,0:T(8,128)(2,1)}, u32[]{:S(2)}, u32[]{:S(2)}) collective-permute-start(bf16[3584,1024]{1,0:T(8,128)(2,1)} %bitcast.18), channel_id=1, source_target_pairs={{0,1},{1,0},{2,3},{3,2},{4,5},{5,4},{6,7},{7,6},{8,9},{9,8},{10,11... | collective-permute-start | bytes 22020104 | tf_op jit(solution)/shard_map/ppermute | solution.py:288
  8.2 64.4 %all-to-all-start = ((bf16[16,16,4480]{2,1,0:T(8,128)(2,1)}), bf16[16,16,4480]{2,1,0:T(8,128)(2,1)S(1)}, u32[]{:S(2)}, u32[]{:S(2)}) async-start(bf16[16,16,4480]{2,1,0:T(8,128)(2,1)} %bitcast.22), calls=%async_computation | async-start | bytes 4587520 | tf_op jit(solution)/shard_map/all_to_all | solution.py:300
  17.2 30.1 %collective-permute-start.2 = (bf16[512,3584]{1,0:T(8,128)(2,1)}, bf16[512,3584]{1,0:T(8,128)(2,1)}, u32[]{:S(2)}, u32[]{:S(2)}) collective-permute-start(bf16[512,3584]{1,0:T(8,128)(2,1)} %bitcast.20), channel_id=1, source_target_pairs={{0,1},{1,0},{2,3},{3,2},{4,5},{5,4},{6,7},{7,6},{8,9},{9,8},{10,11... | collective-permute-start | bytes 11010056 | tf_op jit(solution)/shard_map/ppermute | solution.py:288
  17.6 29.7 %collective-permute-start = (bf16[144,3584]{1,0:T(8,128)(2,1)}, bf16[144,3584]{1,0:T(8,128)(2,1)S(1)}, u32[]{:S(2)}, u32[]{:S(2)}) collective-permute-start(bf16[144,3584]{1,0:T(8,128)(2,1)} %get-tuple-element.33), channel_id=1, source_target_pairs={{0,32},{1,225},{2,34},{3,227},{4,36},{5,229},{6,38},{7,231},{8,40}... | collective-permute-start | bytes 3096584 | tf_op jit(solution)/shard_map/ppermute | solution.py:288
  84.9 12.3 %collective-permute-start.3 = (bf16[16,4480]{1,0:T(8,128)(2,1)S(1)}, bf16[16,4480]{1,0:T(8,128)(2,1)S(1)}, u32[]{:S(2)}, u32[]{:S(2)}) collective-permute-start(bf16[16,4480]{1,0:T(8,128)(2,1)S(1)} %get-tuple-element.42), channel_id=1, source_target_pairs={{0,60},{1,253},{2,62},{3,255},{4,32},{5,225},{6,34},{7,227},{8,36}... | collective-permute-start | bytes 430088 | tf_op jit(solution)/shard_map/ppermute | solution.py:288
  87.3 16.1 %collective-permute-start.4 = (bf16[16,4480]{1,0:T(8,128)(2,1)S(1)}, bf16[16,4480]{1,0:T(8,128)(2,1)S(1)}, u32[]{:S(2)}, u32[]{:S(2)}) collective-permute-start(bf16[16,4480]{1,0:T(8,128)(2,1)S(1)} %get-tuple-element.43), channel_id=1, source_target_pairs={{0,50},{1,243},{2,48},{3,241},{4,54},{5,247},{6,52},{7,245},{8,58}... | collective-permute-start | bytes 430088 | tf_op jit(solution)/shard_map/ppermute | solution.py:288
  93.0 13.2 %collective-permute-start.5 = (bf16[16,4480]{1,0:T(8,128)(2,1)S(1)}, bf16[16,4480]{1,0:T(8,128)(2,1)S(1)}, u32[]{:S(2)}, u32[]{:S(2)}) collective-permute-start(bf16[16,4480]{1,0:T(8,128)(2,1)S(1)} %get-tuple-element.44), channel_id=1, source_target_pairs={{0,36},{1,229},{2,38},{3,231},{4,40},{5,233},{6,42},{7,235},{8,44}... | collective-permute-start | bytes 430088 | tf_op jit(solution)/shard_map/ppermute | solution.py:288
  93.0 16.6 %collective-permute-start.6 = (bf16[16,4480]{1,0:T(8,128)(2,1)S(1)}, bf16[16,4480]{1,0:T(8,128)(2,1)S(1)}, u32[]{:S(2)}, u32[]{:S(2)}) collective-permute-start(bf16[16,4480]{1,0:T(8,128)(2,1)S(1)} %get-tuple-element.45), channel_id=1, source_target_pairs={{0,52},{1,245},{2,54},{3,247},{4,56},{5,249},{6,58},{7,251},{8,60}... | collective-permute-start | bytes 430088 | tf_op jit(solution)/shard_map/ppermute | solution.py:288
  94.7 17.6 %collective-permute-start.7 = (bf16[16,4480]{1,0:T(8,128)(2,1)S(1)}, bf16[16,4480]{1,0:T(8,128)(2,1)S(1)}, u32[]{:S(2)}, u32[]{:S(2)}) collective-permute-start(bf16[16,4480]{1,0:T(8,128)(2,1)S(1)} %get-tuple-element.46), channel_id=1, source_target_pairs={{0,34},{1,227},{2,32},{3,225},{4,38},{5,231},{6,36},{7,229},{8,42}... | collective-permute-start | bytes 430088 | tf_op jit(solution)/shard_map/ppermute | solution.py:288
  97.3 21.1 %collective-permute-start.8 = (bf16[16,4480]{1,0:T(8,128)(2,1)S(1)}, bf16[16,4480]{1,0:T(8,128)(2,1)S(1)}, u32[]{:S(2)}, u32[]{:S(2)}) collective-permute-start(bf16[16,4480]{1,0:T(8,128)(2,1)S(1)} %get-tuple-element.47), channel_id=1, source_target_pairs={{0,44},{1,237},{2,46},{3,239},{4,48},{5,241},{6,50},{7,243},{8,52}... | collective-permute-start | bytes 430088 | tf_op jit(solution)/shard_map/ppermute | solution.py:288
  103.4 15.0 %collective-permute-start.9 = (bf16[16,4480]{1,0:T(8,128)(2,1)S(1)}, bf16[16,4480]{1,0:T(8,128)(2,1)S(1)}, u32[]{:S(2)}, u32[]{:S(2)}) collective-permute-start(bf16[16,4480]{1,0:T(8,128)(2,1)S(1)} %get-tuple-element.48), channel_id=1, source_target_pairs={{0,56},{1,249},{2,58},{3,251},{4,60},{5,253},{6,62},{7,255},{8,32}... | collective-permute-start | bytes 430088 | tf_op jit(solution)/shard_map/ppermute | solution.py:288
  106.1 16.5 %collective-permute-start.10 = (bf16[16,4480]{1,0:T(8,128)(2,1)S(1)}, bf16[16,4480]{1,0:T(8,128)(2,1)S(1)}, u32[]{:S(2)}, u32[]{:S(2)}) collective-permute-start(bf16[16,4480]{1,0:T(8,128)(2,1)S(1)} %get-tuple-element.49), channel_id=1, source_target_pairs={{0,42},{1,235},{2,40},{3,233},{4,46},{5,239},{6,44},{7,237},{8,50}... | collective-permute-start | bytes 430088 | tf_op jit(solution)/shard_map/ppermute | solution.py:288
  109.6 15.2 %collective-permute-start.11 = (bf16[16,4480]{1,0:T(8,128)(2,1)S(1)}, bf16[16,4480]{1,0:T(8,128)(2,1)S(1)}, u32[]{:S(2)}, u32[]{:S(2)}) collective-permute-start(bf16[16,4480]{1,0:T(8,128)(2,1)S(1)} %get-tuple-element.50), channel_id=1, source_target_pairs={{0,48},{1,241},{2,50},{3,243},{4,52},{5,245},{6,54},{7,247},{8,56}... | collective-permute-start | bytes 430088 | tf_op jit(solution)/shard_map/ppermute | solution.py:288
  112.2 19.1 %collective-permute-start.12 = (bf16[16,4480]{1,0:T(8,128)(2,1)S(1)}, bf16[16,4480]{1,0:T(8,128)(2,1)S(1)}, u32[]{:S(2)}, u32[]{:S(2)}) collective-permute-start(bf16[16,4480]{1,0:T(8,128)(2,1)S(1)} %get-tuple-element.51), channel_id=1, source_target_pairs={{0,62},{1,255},{2,60},{3,253},{4,34},{5,227},{6,32},{7,225},{8,38}... | collective-permute-start | bytes 430088 | tf_op jit(solution)/shard_map/ppermute | solution.py:288
  118.4 19.7 %collective-permute-start.13 = (bf16[16,4480]{1,0:T(8,128)(2,1)S(1)}, bf16[16,4480]{1,0:T(8,128)(2,1)S(1)}, u32[]{:S(2)}, u32[]{:S(2)}) collective-permute-start(bf16[16,4480]{1,0:T(8,128)(2,1)S(1)} %get-tuple-element.52), channel_id=1, source_target_pairs={{0,38},{1,231},{2,36},{3,229},{4,42},{5,235},{6,40},{7,233},{8,46}... | collective-permute-start | bytes 430088 | tf_op jit(solution)/shard_map/ppermute | solution.py:288
  118.4 19.7 %collective-permute-start.14 = (bf16[16,4480]{1,0:T(8,128)(2,1)}, bf16[16,4480]{1,0:T(8,128)(2,1)S(1)}, u32[]{:S(2)}, u32[]{:S(2)}) collective-permute-start(bf16[16,4480]{1,0:T(8,128)(2,1)} %get-tuple-element.53), channel_id=1, source_target_pairs={{0,54},{1,247},{2,52},{3,245},{4,58},{5,251},{6,56},{7,249},{8,62}... | collective-permute-start | bytes 430088 | tf_op jit(solution)/shard_map/ppermute | solution.py:288
  122.6 15.4 %collective-permute-start.15 = (bf16[16,4480]{1,0:T(8,128)(2,1)}, bf16[16,4480]{1,0:T(8,128)(2,1)S(1)}, u32[]{:S(2)}, u32[]{:S(2)}) collective-permute-start(bf16[16,4480]{1,0:T(8,128)(2,1)} %get-tuple-element.54), channel_id=1, source_target_pairs={{0,46},{1,239},{2,44},{3,237},{4,50},{5,243},{6,48},{7,241},{8,54}... | collective-permute-start | bytes 430088 | tf_op jit(solution)/shard_map/ppermute | solution.py:288
  124.8 19.3 %collective-permute-start.16 = (bf16[16,4480]{1,0:T(8,128)(2,1)}, bf16[16,4480]{1,0:T(8,128)(2,1)S(1)}, u32[]{:S(2)}, u32[]{:S(2)}) collective-permute-start(bf16[16,4480]{1,0:T(8,128)(2,1)} %get-tuple-element.55), channel_id=1, source_target_pairs={{0,58},{1,251},{2,56},{3,249},{4,62},{5,255},{6,60},{7,253},{8,34}... | collective-permute-start | bytes 430088 | tf_op jit(solution)/shard_map/ppermute | solution.py:288
  131.3 12.8 %collective-permute-start.17 = (bf16[16,4480]{1,0:T(8,128)(2,1)}, bf16[16,4480]{1,0:T(8,128)(2,1)S(1)}, u32[]{:S(2)}, u32[]{:S(2)}) collective-permute-start(bf16[16,4480]{1,0:T(8,128)(2,1)} %get-tuple-element.56), channel_id=1, source_target_pairs={{0,40},{1,233},{2,42},{3,235},{4,44},{5,237},{6,46},{7,239},{8,48}... | collective-permute-start | bytes 430088 | tf_op jit(solution)/shard_map/ppermute | solution.py:288
  138.0 6.3 %collective-permute-start.18 = (bf16[16,4480]{1,0:T(8,128)(2,1)S(1)}, bf16[16,4480]{1,0:T(8,128)(2,1)S(1)}, u32[]{:S(2)}, u32[]{:S(2)}) collective-permute-start(bf16[16,4480]{1,0:T(8,128)(2,1)S(1)} %get-tuple-element.57), channel_id=1, source_target_pairs={{0,32},{1,225},{2,34},{3,227},{4,36},{5,229},{6,38},{7,231},{8,40}... | collective-permute-start | bytes 430088 | tf_op jit(solution)/shard_map/ppermute | solution.py:288
  145.3 6.2 %collective-permute-start.19 = (bf16[64,1792]{1,0:T(8,128)(2,1)S(1)}, bf16[64,1792]{1,0:T(8,128)(2,1)S(1)}, u32[]{:S(2)}, u32[]{:S(2)}) collective-permute-start(bf16[64,1792]{1,0:T(8,128)(2,1)S(1)} %shard_map.88), channel_id=1, source_target_pairs={{0,192},{1,65},{2,194},{3,67},{4,196},{5,69},{6,198},{7,71},{8,200... | collective-permute-start | bytes 688136 | tf_op jit(solution)/shard_map/ppermute | solution.py:288
  146.4 7.5 %collective-permute-start.20 = (bf16[64,1792]{1,0:T(8,128)(2,1)S(1)}, bf16[64,1792]{1,0:T(8,128)(2,1)S(1)}, u32[]{:S(2)}, u32[]{:S(2)}) collective-permute-start(bf16[64,1792]{1,0:T(8,128)(2,1)S(1)} %shard_map.89), channel_id=1, source_target_pairs={{0,192},{1,65},{2,194},{3,67},{4,196},{5,69},{6,198},{7,71},{8,200... | collective-permute-start | bytes 688136 | tf_op jit(solution)/shard_map/ppermute | solution.py:288
